TPU v7x, 32 devices: a whole 2x2x4 slice. The times are simulated.
32 devices in a mesh: ctx: 8 (over y, x, core), tp: 4 (over z).
Axes of the slice: x: 2, y: 2, z: 4, core: 2. Of those that a mesh axis runs over, the one named last changes fastest.
Arguments:
- token_ids: int32 [1024], P('ctx'), may hold values from 0 to 511
- embed_table: bfloat16 [512, 8192], P(None, 'tp'), may hold values from -6 to 6
- query_feat: bfloat16 [1024, 8192], P('ctx', 'tp'), may hold values from -6 to 6
- key_feat: bfloat16 [1024, 8192], P('ctx', 'tp'), may hold values from -6 to 6
- value_feat: bfloat16 [1024, 8192], P('ctx', 'tp'), may hold values from -6 to 6
- long_filter: bfloat16 [1024, 8192], P('ctx', 'tp'), may hold values from -1.45236875 to 1.45236875
- skip_gain: float32 [8192], P('tp'), may hold values from -1 to 1
- norm_gain: bfloat16 [8192], P('tp'), may hold values from 0.099609375 to 1.8984375
- circulant_up: bfloat16 [64, 16, 512], P('tp'), may hold values from -0.0625 to 0.0625
- circulant_down: bfloat16 [16, 64, 512], P(None, 'tp'), may hold values from -0.046875 to 0.046875
Outputs:
- block_out: bfloat16 [1024, 8192], P('ctx', 'tp')
All inputs are finite; a program needn't handle non-finite values.
Results may differ from a plain program's by a relative error of at most 0.01.
Values may be sent and summed in bfloat16 or wider, within the bound.
A program may use at most 128 MiB of HBM per device.

v0:
```python
import functools
import math

import jax
import jax.numpy as jnp
import numpy as np
from jax import lax
from jax.experimental import pallas as pl
from jax.experimental.pallas import tpu as pltpu
from jax.sharding import PartitionSpec as P

D = 8192
BLOCK = 512
HALF = BLOCK // 2
LANES = 128
DENSE_WINDOW = 2048


precise = lax.Precision.HIGHEST
full_turn = 6.283185307179586


def angles(first, second, period, offset):
    left_index = lax.broadcasted_iota(jnp.int32, (first, second), 0)
    right_index = lax.broadcasted_iota(jnp.int32, (first, second), 1) + offset
    return full_turn / period * (left_index * right_index % period).astype(jnp.float32)


def placed(table, layout):
    shape = []
    for letter in layout:
        if letter == "k":
            shape.append(table.shape[0])
        elif letter == "m":
            shape.append(table.shape[1])
        else:
            shape.append(1)
    return table.reshape(shape)


def contract(layout, values, table, source, target):
    result = layout.replace(source, target)
    return jnp.einsum(
        layout + "," + source + target + "->" + result, values, table, precision=precise
    )


def forward_outer(values, layout, offset, period):
    outer = values.shape[layout.index("p")]
    inner = values.shape[layout.index("m")]
    table = angles(outer, 2 * outer, 2 * outer, 0)
    widened = values.astype(jnp.float32)
    real_part = contract(layout, widened, jnp.cos(table), "p", "k")
    imag_part = -contract(layout, widened, jnp.sin(table), "p", "k")
    turned = layout.replace("p", "k")
    twist = angles(2 * outer, inner, period, offset)
    cosine = placed(jnp.cos(twist), turned)
    sine = placed(jnp.sin(twist), turned)
    return (real_part * cosine + imag_part * sine, imag_part * cosine - real_part * sine)


def forward_inner(real_part, imag_part, layout):
    inner = real_part.shape[layout.index("m")]
    table = angles(inner, inner, inner, 0)
    cosine = jnp.cos(table)
    sine = jnp.sin(table)
    new_real = contract(layout, real_part, cosine, "m", "n") + contract(
        layout, imag_part, sine, "m", "n"
    )
    new_imag = contract(layout, imag_part, cosine, "m", "n") - contract(
        layout, real_part, sine, "m", "n"
    )
    return (new_real, new_imag)


def inverse_inner(real_part, imag_part, layout):
    inner = real_part.shape[layout.index("m")]
    table = angles(inner, inner, inner, 0)
    cosine = jnp.cos(table)
    sine = jnp.sin(table)
    new_real = contract(layout, real_part, cosine, "m", "n") - contract(
        layout, imag_part, sine, "m", "n"
    )
    new_imag = contract(layout, imag_part, cosine, "m", "n") + contract(
        layout, real_part, sine, "m", "n"
    )
    return (new_real, new_imag)


def inverse_outer(real_part, imag_part, layout, offset, period):
    doubled = real_part.shape[layout.index("k")]
    inner = real_part.shape[layout.index("m")]
    twist = angles(doubled, inner, period, offset)
    cosine = placed(jnp.cos(twist), layout)
    sine = placed(jnp.sin(twist), layout)
    turned_real = real_part * cosine - imag_part * sine
    turned_imag = imag_part * cosine + real_part * sine
    table = angles(doubled, doubled // 2, doubled, 0)
    summed = contract(layout, turned_real, jnp.cos(table), "k", "p") - contract(
        layout, turned_imag, jnp.sin(table), "k", "p"
    )
    return summed / period


def spectral_product(real_part, imag_part):
    real_out = real_part[0] * real_part[1] - imag_part[0] * imag_part[1]
    imag_out = real_part[0] * imag_part[1] + imag_part[0] * real_part[1]
    return (real_out, imag_out)


def packed_dft(size, rows):
    half = size // 2
    turn = (np.arange(rows)[:, None] * np.arange(half)[None, :]) % size
    angle = 2.0 * np.pi / size * turn
    cosine = np.cos(angle)
    sine = -np.sin(angle)
    sine[:, 0] = 1.0 - 2.0 * (np.arange(rows) % 2)
    return cosine, sine


def packed_weights(size):
    half = size // 2
    weight = np.full((half,), 2.0 / size)
    weight[0] = 1.0 / size
    return weight


def block_tables():
    cosine, sine = packed_dft(BLOCK, BLOCK)
    forward = np.concatenate([cosine, sine], axis=1)
    weight = packed_weights(BLOCK)
    inverse = np.concatenate([cosine * weight, sine * weight], axis=1).T
    cross = sine.copy()
    cross[:, 0] = 0.0
    straight = cosine.copy()
    straight[:, 0] = sine[:, 0]
    taps = np.concatenate([cross, cosine + cross, straight - cross], axis=1)
    return (
        jnp.asarray(forward, jnp.bfloat16),
        jnp.asarray(inverse, jnp.bfloat16),
        jnp.asarray(taps, jnp.bfloat16),
    )


def short_window(signal, kernel):
    length, width = signal.shape
    cosine, sine = packed_dft(2 * length, length)
    table = jnp.asarray(np.concatenate([cosine, sine], axis=1).T, jnp.bfloat16)
    both = jnp.concatenate([signal, kernel], axis=1)
    spectrum = jnp.dot(table, both, preferred_element_type=jnp.float32)
    real_s, real_k = spectrum[:length, :width], spectrum[:length, width:]
    imag_s, imag_k = spectrum[length:, :width], spectrum[length:, width:]
    first = lax.broadcasted_iota(jnp.int32, (length, 1), 0) == 0
    weight = jnp.asarray(packed_weights(2 * length)[:, None], jnp.float32)
    crossed = imag_s * imag_k
    real_out = weight * (real_s * real_k - jnp.where(first, 0.0, crossed))
    imag_out = weight * jnp.where(first, crossed, real_s * imag_k + imag_s * real_k)
    product = jnp.concatenate([real_out, imag_out], axis=0).astype(jnp.bfloat16)
    return lax.dot_general(
        table, product, (((0,), (0,)), ((), ())), preferred_element_type=jnp.float32
    )


def long_window(signal, kernel, outer):
    period = 2 * signal.shape[0]
    tokens = signal.shape[0] // outer
    stacked = jnp.stack([signal, kernel]).reshape(2, outer, tokens, -1).transpose(0, 3, 1, 2)
    real_part, imag_part = forward_outer(stacked, "scpm", 0, period)
    real_part, imag_part = forward_inner(real_part, imag_part, "sckm")
    real_part, imag_part = spectral_product(real_part, imag_part)
    real_part, imag_part = inverse_inner(real_part, imag_part, "ckm")
    local_mixed = inverse_outer(real_part, imag_part, "ckm", 0, period)
    return local_mixed.transpose(1, 2, 0).reshape(outer * tokens, -1)


def mix_blocks(tokens, outs, ins, chunk, real_ref, imag_ref, sum_ref, w_ref, spec_ref, row_of):
    for half in range(HALF // LANES):
        lanes = pl.ds(half * LANES, LANES)

        @pl.loop(0, outs // 2)
        def _(pair):
            def step(part, totals):
                totals = list(totals)
                for inner in range(chunk):
                    if inner % 8 == 0:
                        held = [
                            [
                                w_ref[
                                    pl.ds(pl.multiple_of(row_of(pair * 2 + b, part, inner), 8), 8),
                                    k * HALF + half * LANES : k * HALF + (half + 1) * LANES,
                                ]
                                for k in range(3)
                            ]
                            for b in range(2)
                        ]
                    rows = pl.ds(pl.multiple_of((part * chunk + inner) * tokens, tokens), tokens)
                    real = real_ref[rows, lanes]
                    imag = imag_ref[rows, lanes]
                    both = sum_ref[rows, lanes]
                    at = inner % 8
                    for b in range(2):
                        w0, w1, w2 = [held[b][k][at : at + 1] for k in range(3)]
                        totals[3 * b] = totals[3 * b] + w0 * both
                        totals[3 * b + 1] = totals[3 * b + 1] + w1 * real
                        totals[3 * b + 2] = totals[3 * b + 2] + w2 * imag
                return tuple(totals)

            zero = jnp.zeros((tokens, LANES), jnp.float32)
            totals = (zero,) * 6
            if ins == chunk:
                totals = step(0, totals)
            else:
                totals = lax.fori_loop(0, ins // chunk, step, totals)
            for b in range(2):
                rows = pl.ds(pl.multiple_of((pair * 2 + b) * tokens, tokens), tokens)
                cross, real, imag = totals[3 * b : 3 * b + 3]
                spec_ref[rows, half * LANES : (half + 1) * LANES] = (real - cross).astype(
                    jnp.bfloat16
                )
                spec_ref[rows, HALF + half * LANES : HALF + (half + 1) * LANES] = (
                    cross + imag
                ).astype(jnp.bfloat16)


def mlp_kernel(
    tiles,
    x_ref,
    gain_ref,
    w_ref,
    fwd_ref,
    inv_ref,
    out_ref,
    rows_ref,
    hid_ref,
    spec_ref,
    real_ref,
    imag_ref,
    sum_ref,
):
    groups, tokens, width = x_ref.shape
    per_group = width // BLOCK
    ins = groups * per_group
    stride = w_ref.shape[0] // groups
    local = tiles // groups
    squares = jnp.zeros((tokens, 1), jnp.float32)
    for p in range(groups):
        wide = x_ref[p].astype(jnp.float32)
        squares = squares + jnp.sum(wide * wide, axis=1, keepdims=True)
    scale = lax.rsqrt(squares / (groups * width) + 1e-06)
    for j in range(ins):
        p, at = j // per_group, (j % per_group) * BLOCK
        wide = x_ref[p, :, at : at + BLOCK].astype(jnp.float32)
        gain = gain_ref[j : j + 1, :].astype(jnp.float32)
        rows_ref[j * tokens : (j + 1) * tokens, :] = (wide * scale * gain).astype(jnp.bfloat16)

    piece = 256

    def forward(values_ref, total):
        @pl.loop(0, total // piece)
        def _(at):
            rows = pl.ds(pl.multiple_of(at * piece, piece), piece)
            spec = jnp.dot(values_ref[rows, :], fwd_ref[...], preferred_element_type=jnp.float32)
            real_ref[rows, :] = spec[:, :HALF]
            imag_ref[rows, :] = spec[:, HALF:]
            sum_ref[rows, :] = spec[:, :HALF] + spec[:, HALF:]

    forward(rows_ref, ins * tokens)

    def up_row(i, part, inner):
        return (i // local) * stride + (i % local) * ins + inner

    mix_blocks(tokens, tiles, ins, ins, real_ref, imag_ref, sum_ref, w_ref, spec_ref, up_row)

    @pl.loop(0, tiles * tokens // piece)
    def _(at):
        rows = pl.ds(pl.multiple_of(at * piece, piece), piece)
        pre = jnp.dot(spec_ref[rows, :], inv_ref[...], preferred_element_type=jnp.float32)
        hidden = 0.5 * pre * (1.0 + lax.erf(pre * math.sqrt(0.5)))
        hid_ref[rows, :] = hidden.astype(jnp.bfloat16)

    forward(hid_ref, tiles * tokens)

    def down_row(i, part, inner):
        return part * stride + local * ins + i * local + inner

    mix_blocks(tokens, ins, tiles, local, real_ref, imag_ref, sum_ref, w_ref, spec_ref, down_row)
    for i in range(ins):
        p, at = i // per_group, (i % per_group) * BLOCK
        branch = jnp.dot(
            spec_ref[i * tokens : (i + 1) * tokens, :],
            inv_ref[...],
            preferred_element_type=jnp.float32,
        )
        wide = x_ref[p, :, at : at + BLOCK].astype(jnp.float32)
        out_ref[p, :, at : at + BLOCK] = (wide + branch).astype(jnp.bfloat16)


def mlp(stream, gain, taps, tiles, forward_table, inverse_table):
    groups, tokens, width = stream.shape
    total = tiles * tokens
    wide = pltpu.VMEM((total, HALF), jnp.float32)
    return pl.pallas_call(
        functools.partial(mlp_kernel, tiles),
        out_shape=jax.ShapeDtypeStruct(stream.shape, jnp.bfloat16),
        in_specs=[pl.BlockSpec(memory_space=pltpu.VMEM)] * 5,
        out_specs=pl.BlockSpec(memory_space=pltpu.VMEM),
        scratch_shapes=[
            pltpu.VMEM((groups * width // BLOCK * tokens, BLOCK), jnp.bfloat16),
            pltpu.VMEM((total, BLOCK), jnp.bfloat16),
            pltpu.VMEM((total, BLOCK), jnp.bfloat16),
            wide,
            wide,
            wide,
        ],
        compiler_params=pltpu.CompilerParams(vmem_limit_bytes=40 * 1024 * 1024),
        name="circulant_mlp",
    )(stream, gain, taps, forward_table, inverse_table)


def body(
    token_ids,
    embed_table,
    query_feat,
    key_feat,
    value_feat,
    long_filter,
    skip_gain,
    norm_gain,
    circulant_up,
    circulant_down,
):
    tokens = token_ids.shape[0]
    vocab = embed_table.shape[0]
    outer = lax.axis_size("ctx")
    groups = lax.axis_size("tp")
    width = query_feat.shape[1]
    ins = circulant_up.shape[1]
    local = circulant_up.shape[0]
    gated_wide = key_feat.astype(jnp.float32) * value_feat.astype(jnp.float32)
    gated = gated_wide.astype(jnp.bfloat16)
    arrived_signal, arrived_kernel = (
        lax.all_to_all(gated, "ctx", split_axis=1, concat_axis=0, tiled=True),
        lax.all_to_all(long_filter, "ctx", split_axis=1, concat_axis=0, tiled=True),
    )
    forward_table, inverse_table, tap_table = block_tables()
    gain_rows = norm_gain.reshape(-1, BLOCK)
    padded = 16
    gain_rows = jnp.pad(gain_rows, ((0, padded - gain_rows.shape[0]), (0, 0)))
    columns = jnp.concatenate(
        [circulant_up.reshape(-1, BLOCK), circulant_down.reshape(-1, BLOCK), gain_rows], axis=0
    )
    all_columns = lax.all_gather(columns, "tp", axis=0, tiled=True)
    taps = jnp.dot(all_columns, tap_table, preferred_element_type=jnp.float32)
    full_gain = all_columns.reshape(groups, -1, BLOCK)[:, -padded : width // BLOCK - padded, :]
    full_gain = full_gain.reshape(-1, BLOCK)
    onehot = (token_ids[:, None] == lax.broadcasted_iota(jnp.int32, (1, vocab), 1)).astype(
        jnp.bfloat16
    )
    embedded = jnp.dot(onehot, embed_table, preferred_element_type=jnp.float32)
    if outer * tokens <= DENSE_WINDOW:
        local_mixed = short_window(arrived_signal, arrived_kernel)
    else:
        local_mixed = long_window(arrived_signal, arrived_kernel, outer)
    mixed = lax.all_to_all(
        local_mixed.astype(jnp.bfloat16), "ctx", split_axis=0, concat_axis=1, tiled=True
    ).astype(jnp.float32)
    mixed = mixed + skip_gain[None, :] * gated.astype(jnp.float32)
    stream = (embedded + query_feat.astype(jnp.float32) * mixed).astype(jnp.bfloat16)
    own = lax.all_to_all(
        stream.reshape(groups, tokens // groups, width), "tp", split_axis=0, concat_axis=0
    )
    result = mlp(own, full_gain, taps, local * groups, forward_table, inverse_table)
    return lax.all_to_all(result, "tp", split_axis=0, concat_axis=0).reshape(tokens, width)


def solution(mesh):
    placed = (
        P("ctx"),
        P(None, "tp"),
        P("ctx", "tp"),
        P("ctx", "tp"),
        P("ctx", "tp"),
        P("ctx", "tp"),
        P("tp"),
        P("tp"),
        P("tp", None, None),
        P(None, "tp", None),
    )
    return jax.shard_map(
        body, mesh=mesh, in_specs=placed, out_specs=P("ctx", "tp"), check_vma=False
    )
```

profile of v0, /device:TPU:0, one launch (start us, length us, event | category | flops | bytes accessed | tf_op | source)
XLA Modules:
  0.0 133.7 jit_solution(11908246146576303820)
XLA Ops:
  6.5 0.0 copy-start
  6.5 0.0 copy-start.8
  6.5 0.0 copy-start.5
  6.5 0.0 copy-start.6
  6.5 2.2 %copy.24 = bf16[128,2048]{0,1:T(8,128)(2,1)} copy(bf16[128,2048]{1,0:T(8,128)(2,1)} %param.20) | data formatting | bytes 1048576 | tf_op args[5]
  8.7 5.2 %all-to-all-start.1 = ((bf16[128,8,256]{0,2,1:T(8,128)(2,1)}), bf16[128,8,256]{0,2,1:T(8,128)(2,1)S(1)}, u32[]{:S(2)}, u32[]{:S(2)}) async-start(bf16[128,8,256]{0,2,1:T(8,128)(2,1)} %bitcast.2), calls=%async_computation.1 | async-start | bytes 1048576 | tf_op jit(solution)/shard_map/all_to_all | solution.py:343
  13.9 0.0 all-gather.2.cloned.1.call-start
  13.9 0.0 copy-done.8
  14.0 0.0 copy-done.5
  14.0 0.0 copy-done.6
  14.0 0.8 fusion.8
  14.8 0.0 all-gather.2.cloned.1.call-update
  14.9 1.3 multiply_convert_fusion.2
  16.2 0.8 copy.32
  17.0 6.6 %all-to-all-done.1 = bf16[128,8,256]{0,2,1:T(8,128)(2,1)S(1)} async-done(((bf16[128,8,256]{0,2,1:T(8,128)(2,1)}), bf16[128,8,256]{0,2,1:T(8,128)(2,1)S(1)}, u32[]{:S(2)}, u32[]{:S(2)}) %all-to-all-start.1) | async-done | bytes 524320 | tf_op jit(solution)/shard_map/all_to_all | solution.py:343
  23.6 4.1 %all-to-all-start = ((bf16[128,8,256]{2,0,1:T(8,128)(2,1)}), bf16[128,8,256]{2,0,1:T(8,128)(2,1)}, u32[]{:S(2)}, u32[]{:S(2)}) async-start(bf16[128,8,256]{2,0,1:T(8,128)(2,1)} %bitcast.32), calls=%async_computation | async-start | bytes 1048576 | tf_op jit(solution)/shard_map/all_to_all | solution.py:342
  27.8 1.0 copy.25
  28.8 8.7 %all-to-all-done = bf16[128,8,256]{2,0,1:T(8,128)(2,1)} async-done(((bf16[128,8,256]{2,0,1:T(8,128)(2,1)}), bf16[128,8,256]{2,0,1:T(8,128)(2,1)}, u32[]{:S(2)}, u32[]{:S(2)}) %all-to-all-start) | async-done | bytes 524320 | tf_op jit(solution)/shard_map/all_to_all | solution.py:342
  37.6 0.0 copy-start.11
  37.6 0.0 copy-start.12
  37.6 5.0 %fusion.4 = f32[2048,512]{1,0:T(8,128)S(1)} fusion(bf16[2048,1024]{1,0:T(8,128)(2,1)} %constant.20.clone, bf16[1024,256]{1,0:T(8,128)(2,1)} %bitcast.35, bf16[1024,256]{1,0:T(8,128)(2,1)} %bitcast.1), kind=kOutput, calls=%fused_computation.7 | convolution fusion | flops 2149580800 | bytes 9437184 | tf_op jit(solution)/shard_map/dot_general | solution.py:150
  42.6 0.0 copy-done.11
  42.6 0.0 copy-done.12
  42.6 0.0 copy-start.10
  42.6 1.1 fusion.11
  43.7 0.5 copy-done.10
  44.2 1.9 %fusion.2 = bf16[1024,256]{0,1:T(8,128)(2,1)} fusion(f32[256,1024]{1,0:T(8,128)S(1)} %fusion.11, bf16[1024,1024]{1,0:T(8,128)(2,1)S(1)} %copy-done.10, f32[2048,512]{1,0:T(8,128)S(1)} %fusion.4, f32[1024]{0:T(1024)S(1)} %copy-done.12, pred[1024]{0:T(1024)(128)(4,1)S(1)} %iota_compare_fusion.3), kind=kOutput, calls=%fused_computation.4 | convolution fusion | flops 539230208 | bytes 7869440 | tf_op jit(solution)/shard_map/dot_general | solution.py:159
  46.1 1.2 copy.28
  47.3 12.2 %all_to_all.61 = bf16[8,128,256]{2,1,0:T(8,128)(2,1)S(1)} all-to-all(bf16[8,128,256]{2,1,0:T(8,128)(2,1)S(1)} %bitcast.33), channel_id=1, replica_groups=mesh['ctx'=8,'tp'=4] {'ctx'}, dimensions={0} | all-to-all | bytes 1048576 | tf_op jit(solution)/shard_map/all_to_all | solution.py:364
  59.5 0.0 copy-start.4
  59.5 0.0 copy-start.7
  59.5 0.0 copy-start.9
  59.5 0.1 convert_bitcast_fusion
  59.6 0.1 copy.30
  59.7 0.0 copy-done
  59.7 0.8 copy-done.4
  60.5 0.0 copy-done.7
  60.5 0.0 copy-done.9
  60.5 1.4 %fusion = bf16[128,2048]{1,0:T(8,128)(2,1)} fusion(bf16[512,2048]{1,0:T(8,128)(2,1)S(1)} %copy-done, f32[128,2048]{1,0:T(8,128)S(1)} %bitcast.29, bf16[128,2048]{1,0:T(8,128)(2,1)S(1)} %multiply_convert_fusion.2, bf16[128,2048]{1,0:T(8,128)(2,1)S(1)} %copy-done.4, f32[2048]{0:T(1024)S(1)} %copy-done.7, s32[128]{0:T(128)S(1)} %copy-done.9), kind=kOutput, calls=%fused_computation.1 | convolution fusion | flops 270336000 | bytes 4727296 | tf_op jit(solution)/shard_map/dot_general | solution.py:359
  62.0 4.9 %all-to-all-start.3 = ((bf16[4,32,2048]{2,1,0:T(8,128)(2,1)}), bf16[4,32,2048]{2,1,0:T(8,128)(2,1)S(1)}, u32[]{:S(2)}, u32[]{:S(2)}) async-start(bf16[4,32,2048]{2,1,0:T(8,128)(2,1)} %bitcast.8), calls=%async_computation.3 | async-start | bytes 1048576 | tf_op jit(solution)/shard_map/all_to_all | solution.py:369
  66.9 0.0 all-gather.2.cloned.1.call-done
  66.9 0.8 slice.26
  67.6 0.0 copy-start.2
  67.7 6.4 %fusion.15.w_ref = f32[2112,768]{1,0:T(8,128)} fusion(bf16[2112,512]{1,0:T(8,128)(2,1)} %all-gather.2.cloned.1.call-done, bf16[512,768]{1,0:T(8,128)(2,1)} %constant.19.clone), kind=kOutput, calls=%fused_computation.26 | convolution fusion | flops 1660944384 | bytes 9437184 | tf_op jit(solution)/shard_map/dot_general | solution.py:353
  74.0 6.8 %all-to-all-done.3.x_ref = bf16[4,32,2048]{2,1,0:T(8,128)(2,1)S(1)} async-done(((bf16[4,32,2048]{2,1,0:T(8,128)(2,1)}), bf16[4,32,2048]{2,1,0:T(8,128)(2,1)S(1)}, u32[]{:S(2)}, u32[]{:S(2)}) %all-to-all-start.3) | async-done | bytes 524320 | tf_op jit(solution)/shard_map/all_to_all | solution.py:369
  80.8 0.0 copy-done.2
  80.8 0.0 copy-start.1
  80.8 2.8 %copy-done.1 = f32[2112,768]{1,0:T(8,128)S(1)} copy-done((f32[2112,768]{1,0:T(8,128)S(1)}, f32[2112,768]{1,0:T(8,128)}, u32[]{:S(2)}) %copy-start.1) | copy-done | bytes 6488088
  83.7 0.0 copy-start.3
  83.7 1.0 copy-done.3
  84.7 25.0 %circulant_mlp.1 = bf16[4,32,2048]{2,1,0:T(8,128)(2,1)S(1)} custom-call(bf16[4,32,2048]{2,1,0:T(8,128)(2,1)S(1)} %all-to-all-done.3.x_ref, bf16[16,512]{1,0:T(8,128)(2,1)S(1)} %reshape.44.gain_ref, f32[2112,768]{1,0:T(8,128)S(1)} %copy-done.1, bf16[512,512]{1,0:T(8,128)(2,1)S(1)} %copy-done.3, bf16[512,512]{1,0:T(8,128)(2,1)S(1)} %copy-done.2), custom_call_target="tpu_custom_call" | custom-call | tf_op jit(solution)/shard_map/circulant_mlp/pallas_call | solution.py:302
  109.7 16.4 %all_to_all.62 = bf16[4,32,2048]{2,1,0:T(8,128)(2,1)S(1)} all-to-all(bf16[4,32,2048]{2,1,0:T(8,128)(2,1)S(1)} %circulant_mlp.1), channel_id=1, replica_groups=mesh['ctx'=8,'tp'=4] {'tp'}, dimensions={0} | all-to-all | bytes 1048576 | tf_op jit(solution)/shard_map/all_to_all | solution.py:373
  126.0 0.8 copy.34
  (3 shorter events, 0.0 us)
Async XLA Ops:
  6.5 53.2 %copy-start = (bf16[512,2048]{1,0:T(8,128)(2,1)S(1)}, bf16[512,2048]{1,0:T(8,128)(2,1)}, u32[]{:S(2)}) copy-start(bf16[512,2048]{1,0:T(8,128)(2,1)} %param.16) | copy-start | bytes 6291460
  6.5 7.4 %copy-start.8 = (bf16[2048]{0:T(1024)(128)(2,1)S(1)}, bf16[2048]{0:T(1024)(128)(2,1)}, u32[]{:S(2)}) copy-start(bf16[2048]{0:T(1024)(128)(2,1)} %param.22) | copy-start | bytes 12292
  6.5 7.4 %copy-start.5 = (bf16[16,16,512]{2,1,0:T(8,128)(2,1)S(1)}, bf16[16,16,512]{2,1,0:T(8,128)(2,1)}, u32[]{:S(2)}) copy-start(bf16[16,16,512]{2,1,0:T(8,128)(2,1)} %param.24) | copy-start | bytes 786436
  6.5 7.4 %copy-start.6 = (bf16[16,16,512]{2,1,0:T(8,128)(2,1)S(1)}, bf16[16,16,512]{2,1,0:T(8,128)(2,1)}, u32[]{:S(2)}) copy-start(bf16[16,16,512]{2,1,0:T(8,128)(2,1)} %param.23) | copy-start | bytes 786436
  8.7 14.9 %all-to-all-start.1 = ((bf16[128,8,256]{0,2,1:T(8,128)(2,1)}), bf16[128,8,256]{0,2,1:T(8,128)(2,1)S(1)}, u32[]{:S(2)}, u32[]{:S(2)}) async-start(bf16[128,8,256]{0,2,1:T(8,128)(2,1)} %bitcast.2), calls=%async_computation.1 | async-start | bytes 1048576 | tf_op jit(solution)/shard_map/all_to_all | solution.py:343
  13.9 53.0 %all-gather.2.cloned.1.call-start = ((), (), s32[]{:S(2)}) async-start(), calls=%async_computation.5 | async-start | bytes 2703360 | tf_op jit(solution)/shard_map/all_gather | solution.py:352
  23.6 13.9 %all-to-all-start = ((bf16[128,8,256]{2,0,1:T(8,128)(2,1)}), bf16[128,8,256]{2,0,1:T(8,128)(2,1)}, u32[]{:S(2)}, u32[]{:S(2)}) async-start(bf16[128,8,256]{2,0,1:T(8,128)(2,1)} %bitcast.32), calls=%async_computation | async-start | bytes 1048576 | tf_op jit(solution)/shard_map/all_to_all | solution.py:342
  37.6 5.0 %copy-start.11 = (bf16[1024,1024]{1,0:T(8,128)(2,1)S(1)}, bf16[1024,1024]{1,0:T(8,128)(2,1)}, u32[]{:S(2)}) copy-start(bf16[1024,1024]{1,0:T(8,128)(2,1)} %constant.25) | copy-start | bytes 6291460
  37.6 5.0 %copy-start.12 = (f32[1024]{0:T(1024)S(1)}, f32[1024]{0:T(1024)}, u32[]{:S(2)}) copy-start(f32[1024]{0:T(1024)} %constant.24) | copy-start | bytes 12292
  42.6 1.6 %copy-start.10 = (bf16[1024,1024]{1,0:T(8,128)(2,1)S(1)}, bf16[1024,1024]{1,0:T(8,128)(2,1)}, u32[]{:S(2)}) copy-start(bf16[1024,1024]{1,0:T(8,128)(2,1)} %constant.26) | copy-start | bytes 6291460
  59.5 1.0 copy-start.4
  59.5 1.0 copy-start.7
  59.5 1.0 copy-start.9
  62.0 18.8 %all-to-all-start.3 = ((bf16[4,32,2048]{2,1,0:T(8,128)(2,1)}), bf16[4,32,2048]{2,1,0:T(8,128)(2,1)S(1)}, u32[]{:S(2)}, u32[]{:S(2)}) async-start(bf16[4,32,2048]{2,1,0:T(8,128)(2,1)} %bitcast.8), calls=%async_computation.3 | async-start | bytes 1048576 | tf_op jit(solution)/shard_map/all_to_all | solution.py:369
  67.6 13.2 %copy-start.2 = (bf16[512,512]{1,0:T(8,128)(2,1)S(1)}, bf16[512,512]{1,0:T(8,128)(2,1)}, u32[]{:S(2)}) copy-start(bf16[512,512]{1,0:T(8,128)(2,1)} %constant.18.clone.inv_ref) | copy-start | bytes 1572868
  80.8 2.8 %copy-start.1 = (f32[2112,768]{1,0:T(8,128)S(1)}, f32[2112,768]{1,0:T(8,128)}, u32[]{:S(2)}) copy-start(f32[2112,768]{1,0:T(8,128)} %fusion.15.w_ref) | copy-start | bytes 19464196
  83.7 1.0 copy-start.3
Sparse Core Ops, SparseCore 0:
  16.3 48.9 all-gather.1
where the time goes:
time: 134 us
  blocking collectives  28.5 us (21%)
  Pallas kernels  25 us (19%)
  waiting for transfers between devices  22.1 us (16%)
  matrix products  15.8 us (12%)
  starting transfers between devices  14.2 us (11%)
  between operations  13.5 us (10%)
  local copies, waits for them, and re-layouts  12.2 us (9%)
  other arithmetic  2.27 us (2%)
    pallas_call x1, Pallas kernels, mlp(): pl.pallas_call(functools.partial(mlp_kernel, tiles), out_shape=jax.ShapeD...  25 us
    all_to_all x1, blocking collectives, body(): lax.all_to_all(result, 'tp', split_axis=0, concat_axis=0)  16.4 us
    all_to_all x1, blocking collectives, body(): lax.all_to_all(local_mixed.astype(jnp.bfloat16), 'ctx', split_axis=0, con...  12.2 us
    all_to_all x1, waiting for transfers between devices, body(): lax.all_to_all(gated, 'ctx', split_axis=1, concat_axis=0, tiled=True)  8.73 us
    unnamed x28, local copies, waits for them, and re-layouts  8.26 us
    all_to_all x1, waiting for transfers between devices, body(): lax.all_to_all(stream.reshape(groups, tokens // groups, width), 'tp', spl...  6.77 us
    all_to_all x1, waiting for transfers between devices, body(): lax.all_to_all(long_filter, 'ctx', split_axis=1, concat_axis=0, tiled=True)  6.62 us
    dot_general x1, matrix products, body(): taps = jnp.dot(all_columns, tap_table, preferred_element_type=jnp.float32)  6.38 us
  transfers between devices with their start and end apart: 4, of which 3 were waited for; matrix products, arithmetic and copies ran while one was open for 16% of the time, Pallas kernels for 0%

commit v1 on v0

--- a/solution.py
+++ b/solution.py
@@ -142,11 +142,10 @@
     )
 
 
-def short_window(signal, kernel):
-    length, width = signal.shape
+def short_window(both):
+    length, width = both.shape[0], both.shape[1] // 2
     cosine, sine = packed_dft(2 * length, length)
     table = jnp.asarray(np.concatenate([cosine, sine], axis=1).T, jnp.bfloat16)
-    both = jnp.concatenate([signal, kernel], axis=1)
     spectrum = jnp.dot(table, both, preferred_element_type=jnp.float32)
     real_s, real_k = spectrum[:length, :width], spectrum[:length, width:]
     imag_s, imag_k = spectrum[length:, :width], spectrum[length:, width:]
@@ -223,25 +222,68 @@
 
 
 def mlp_kernel(
-    tiles,
-    x_ref,
-    gain_ref,
-    w_ref,
+    local,
+    mine_ref,
+    cols_ref,
     fwd_ref,
     inv_ref,
+    tap_ref,
     out_ref,
+    x_ref,
+    done_ref,
+    w_ref,
     rows_ref,
     hid_ref,
     spec_ref,
     real_ref,
     imag_ref,
     sum_ref,
+    send_sem,
+    recv_sem,
+    back_send_sem,
+    back_recv_sem,
 ):
-    groups, tokens, width = x_ref.shape
+    groups, tokens, width = mine_ref.shape
     per_group = width // BLOCK
     ins = groups * per_group
-    stride = w_ref.shape[0] // groups
-    local = tiles // groups
+    tiles = groups * local
+    stride = 2 * local * ins
+    held = cols_ref.shape[0] // groups
+    me = lax.axis_index("tp")
+    peers = [lax.rem(me + d, groups) for d in range(1, groups)]
+
+    barrier = pltpu.get_barrier_semaphore()
+    for peer in peers:
+        pl.semaphore_signal(
+            barrier, inc=1, device_id={"tp": peer}, device_id_type=pl.DeviceIdType.MESH
+        )
+    pl.semaphore_wait(barrier, groups - 1)
+
+    def send(d, src, dst, sent, got):
+        copy = pltpu.make_async_remote_copy(
+            src_ref=src.at[peers[d]],
+            dst_ref=dst.at[me],
+            send_sem=sent.at[d],
+            recv_sem=got.at[d],
+            device_id={"tp": peers[d]},
+            device_id_type=pl.DeviceIdType.MESH,
+        )
+        copy.start()
+        return copy
+
+    copies = [send(d, mine_ref, x_ref, send_sem, recv_sem) for d in range(groups - 1)]
+    x_ref[me] = mine_ref[me]
+    for p in range(groups):
+        for part in range(2):
+            at = part * local * ins
+            w_ref[p * stride + at : p * stride + at + local * ins, :] = jnp.dot(
+                cols_ref[p * held + at : p * held + at + local * ins, :],
+                tap_ref[...],
+                preferred_element_type=jnp.float32,
+            )
+    for copy in copies:
+        copy.wait()
+
     squares = jnp.zeros((tokens, 1), jnp.float32)
     for p in range(groups):
         wide = x_ref[p].astype(jnp.float32)
@@ -250,7 +292,8 @@
     for j in range(ins):
         p, at = j // per_group, (j % per_group) * BLOCK
         wide = x_ref[p, :, at : at + BLOCK].astype(jnp.float32)
-        gain = gain_ref[j : j + 1, :].astype(jnp.float32)
+        row = p * held + stride + j % per_group
+        gain = cols_ref[row : row + 1, :].astype(jnp.float32)
         rows_ref[j * tokens : (j + 1) * tokens, :] = (wide * scale * gain).astype(jnp.bfloat16)
 
     piece = 256
@@ -280,41 +323,64 @@
 
     forward(hid_ref, tiles * tokens)
 
-    def down_row(i, part, inner):
-        return part * stride + local * ins + i * local + inner
-
-    mix_blocks(tokens, ins, tiles, local, real_ref, imag_ref, sum_ref, w_ref, spec_ref, down_row)
-    for i in range(ins):
-        p, at = i // per_group, (i % per_group) * BLOCK
+    copies = []
+    for d in range(groups):
+        target = peers[d] if d < groups - 1 else me
+
+        def down_row(i, part, inner):
+            return part * stride + local * ins + (target * per_group + i) * local + inner
+
+        mix_blocks(
+            tokens, per_group, tiles, local, real_ref, imag_ref, sum_ref, w_ref, spec_ref, down_row
+        )
         branch = jnp.dot(
-            spec_ref[i * tokens : (i + 1) * tokens, :],
-            inv_ref[...],
-            preferred_element_type=jnp.float32,
+            spec_ref[: per_group * tokens, :], inv_ref[...], preferred_element_type=jnp.float32
         )
-        wide = x_ref[p, :, at : at + BLOCK].astype(jnp.float32)
-        out_ref[p, :, at : at + BLOCK] = (wide + branch).astype(jnp.bfloat16)
-
-
-def mlp(stream, gain, taps, tiles, forward_table, inverse_table):
+        for i in range(per_group):
+            at = i * BLOCK
+            wide = x_ref[target, :, at : at + BLOCK].astype(jnp.float32)
+            total = (wide + branch[i * tokens : (i + 1) * tokens]).astype(jnp.bfloat16)
+            if d < groups - 1:
+                done_ref[target, :, at : at + BLOCK] = total
+            else:
+                out_ref[target, :, at : at + BLOCK] = total
+        if d < groups - 1:
+            copies.append(send(d, done_ref, out_ref, back_send_sem, back_recv_sem))
+    for copy in copies:
+        copy.wait()
+
+
+def mlp(stream, columns, local, forward_table, inverse_table, tap_table):
     groups, tokens, width = stream.shape
-    total = tiles * tokens
+    ins = groups * width // BLOCK
+    total = groups * local * tokens
     wide = pltpu.VMEM((total, HALF), jnp.float32)
+    arrivals = pltpu.SemaphoreType.DMA((groups - 1,))
     return pl.pallas_call(
-        functools.partial(mlp_kernel, tiles),
+        functools.partial(mlp_kernel, local),
         out_shape=jax.ShapeDtypeStruct(stream.shape, jnp.bfloat16),
         in_specs=[pl.BlockSpec(memory_space=pltpu.VMEM)] * 5,
         out_specs=pl.BlockSpec(memory_space=pltpu.VMEM),
         scratch_shapes=[
-            pltpu.VMEM((groups * width // BLOCK * tokens, BLOCK), jnp.bfloat16),
+            pltpu.VMEM(stream.shape, jnp.bfloat16),
+            pltpu.VMEM(stream.shape, jnp.bfloat16),
+            pltpu.VMEM((2 * groups * local * ins, 3 * HALF), jnp.float32),
+            pltpu.VMEM((ins * tokens, BLOCK), jnp.bfloat16),
             pltpu.VMEM((total, BLOCK), jnp.bfloat16),
             pltpu.VMEM((total, BLOCK), jnp.bfloat16),
             wide,
             wide,
             wide,
+            arrivals,
+            arrivals,
+            arrivals,
+            arrivals,
         ],
-        compiler_params=pltpu.CompilerParams(vmem_limit_bytes=40 * 1024 * 1024),
+        compiler_params=pltpu.CompilerParams(
+            vmem_limit_bytes=40 * 1024 * 1024, collective_id=1, has_side_effects=True
+        ),
         name="circulant_mlp",
-    )(stream, gain, taps, forward_table, inverse_table)
+    )(stream, columns, forward_table, inverse_table, tap_table)
 
 
 def body(
@@ -338,10 +404,11 @@
     local = circulant_up.shape[0]
     gated_wide = key_feat.astype(jnp.float32) * value_feat.astype(jnp.float32)
     gated = gated_wide.astype(jnp.bfloat16)
-    arrived_signal, arrived_kernel = (
-        lax.all_to_all(gated, "ctx", split_axis=1, concat_axis=0, tiled=True),
-        lax.all_to_all(long_filter, "ctx", split_axis=1, concat_axis=0, tiled=True),
-    )
+    pairs = jnp.concatenate(
+        [gated.reshape(tokens, outer, -1), long_filter.reshape(tokens, outer, -1)], axis=2
+    )
+    arrived = lax.all_to_all(pairs, "ctx", split_axis=1, concat_axis=0)
+    arrived = arrived.reshape(outer * tokens, -1)
     forward_table, inverse_table, tap_table = block_tables()
     gain_rows = norm_gain.reshape(-1, BLOCK)
     padded = 16
@@ -350,27 +417,22 @@
         [circulant_up.reshape(-1, BLOCK), circulant_down.reshape(-1, BLOCK), gain_rows], axis=0
     )
     all_columns = lax.all_gather(columns, "tp", axis=0, tiled=True)
-    taps = jnp.dot(all_columns, tap_table, preferred_element_type=jnp.float32)
-    full_gain = all_columns.reshape(groups, -1, BLOCK)[:, -padded : width // BLOCK - padded, :]
-    full_gain = full_gain.reshape(-1, BLOCK)
     onehot = (token_ids[:, None] == lax.broadcasted_iota(jnp.int32, (1, vocab), 1)).astype(
         jnp.bfloat16
     )
     embedded = jnp.dot(onehot, embed_table, preferred_element_type=jnp.float32)
     if outer * tokens <= DENSE_WINDOW:
-        local_mixed = short_window(arrived_signal, arrived_kernel)
+        local_mixed = short_window(arrived)
     else:
-        local_mixed = long_window(arrived_signal, arrived_kernel, outer)
+        local_mixed = long_window(*jnp.split(arrived, 2, axis=1), outer)
     mixed = lax.all_to_all(
         local_mixed.astype(jnp.bfloat16), "ctx", split_axis=0, concat_axis=1, tiled=True
     ).astype(jnp.float32)
     mixed = mixed + skip_gain[None, :] * gated.astype(jnp.float32)
     stream = (embedded + query_feat.astype(jnp.float32) * mixed).astype(jnp.bfloat16)
-    own = lax.all_to_all(
-        stream.reshape(groups, tokens // groups, width), "tp", split_axis=0, concat_axis=0
-    )
-    result = mlp(own, full_gain, taps, local * groups, forward_table, inverse_table)
-    return lax.all_to_all(result, "tp", split_axis=0, concat_axis=0).reshape(tokens, width)
+    own = stream.reshape(groups, tokens // groups, width)
+    result = mlp(own, all_columns, local, forward_table, inverse_table, tap_table)
+    return result.reshape(tokens, width)
 
 
 def solution(mesh):

time: 134 us -> 126 us (0.940)
  Pallas kernels: 25 us -> 42.8 us
  blocking collectives: 28.5 us -> 12.2 us
  starting transfers between devices: 14.2 us -> 5.21 us
  matrix products: 15.8 us -> 7.63 us
  waiting for transfers between devices: 22.1 us -> 27.7 us
  other arithmetic: 2.27 us -> 5.44 us
    pallas_call x1, Pallas kernels: 25 us -> 42.8 us  [mlp(): pl.pallas_call(functools.partial(mlp_kernel, local), out_shape=jax.ShapeD...]
    all_to_all x1 -> x0, blocking collectives: 16.4 us -> none  [body(): lax.all_to_all(result, 'tp', split_axis=0, concat_axis=0)]
    all_gather x1, waiting for transfers between devices: 0.01 us -> 14.1 us  [body(): all_columns = lax.all_gather(columns, 'tp', axis=0, tiled=True)]
    all_to_all x3 -> x1, starting transfers between devices: 14.2 us -> 5.17 us  [body(): arrived = lax.all_to_all(pairs, 'ctx', split_axis=1, concat_axis=0)]
    all_to_all x3 -> x1, waiting for transfers between devices: 22.1 us -> 13.5 us  [body(): arrived = lax.all_to_all(pairs, 'ctx', split_axis=1, concat_axis=0)]
    dot_general x1 -> x0, matrix products: 6.38 us -> none  [body(): taps = jnp.dot(all_columns, tap_table, preferred_element_type=jnp.float32)]
    broadcast_in_dim x0 -> x1, local copies, waits for them, and re-layouts: none -> 2.3 us  [body(): arrived = lax.all_to_all(pairs, 'ctx', split_axis=1, concat_axis=0)]
    broadcast_in_dim x0 -> x1, other arithmetic: none -> 2.09 us  [body(): arrived = lax.all_to_all(pairs, 'ctx', split_axis=1, concat_axis=0)]
  transfers between devices with their start and end apart: 4 -> 2, of which waited for: 3 -> 2; matrix products, arithmetic and copies ran while one was open for 16% -> 8% of each run, Pallas kernels for 0% -> 0%
where the time goes in v1:
time: 126 us; the launch traced here: 125 us
  Pallas kernels  42.8 us (34%)
  waiting for transfers between devices  27.7 us (22%)
  between operations  13.5 us (11%)
  blocking collectives  12.2 us (10%)
  local copies, waits for them, and re-layouts  11 us (9%)
  matrix products  7.63 us (6%)
  other arithmetic  5.44 us (4%)
  starting transfers between devices  5.21 us (4%)
    pallas_call x1, Pallas kernels, mlp(): pl.pallas_call(functools.partial(mlp_kernel, local), out_shape=jax.ShapeD...  42.8 us
    all_gather x1, waiting for transfers between devices, body(): all_columns = lax.all_gather(columns, 'tp', axis=0, tiled=True)  14.1 us
    all_to_all x1, waiting for transfers between devices, body(): arrived = lax.all_to_all(pairs, 'ctx', split_axis=1, concat_axis=0)  13.5 us
    all_to_all x1, blocking collectives, body(): lax.all_to_all(local_mixed.astype(jnp.bfloat16), 'ctx', split_axis=0, con...  12.2 us
    unnamed x32, local copies, waits for them, and re-layouts  8.13 us
    all_to_all x1, starting transfers between devices, body(): arrived = lax.all_to_all(pairs, 'ctx', split_axis=1, concat_axis=0)  5.17 us
    dot_general x1, matrix products, short_window(): spectrum = jnp.dot(table, both, preferred_element_type=jnp.float32)  4.91 us
  transfers between devices with their start and end apart: 2, of which 2 were waited for; matrix products, arithmetic and copies ran while one was open for 8% of the time, Pallas kernels for 0%

profile of v1, /device:TPU:0, one launch (start us, length us, event | category | flops | bytes accessed | tf_op | source)
XLA Modules:
  0.0 125.5 jit_solution(12356106705827789424)
XLA Ops:
  6.5 0.0 copy-start
  6.5 1.5 %multiply_convert_fusion.2 = bf16[128,2048]{1,0:T(8,128)(2,1)S(1)} fusion(bf16[128,2048]{1,0:T(8,128)(2,1)} %param.19, bf16[128,2048]{1,0:T(8,128)(2,1)} %param.18), kind=kLoop, calls=%fused_computation.14 | loop fusion | flops 1048576 | bytes 1572864 | tf_op jit(solution)/shard_map/convert_element_type | solution.py:406
  8.0 0.0 copy-start.5
  8.0 0.3 copy.26
  8.3 2.0 %copy.20 = bf16[128,2048]{0,1:T(8,128)(2,1)} copy(bf16[128,2048]{1,0:T(8,128)(2,1)} %param.20) | data formatting | bytes 1048576 | tf_op args[5]
  10.3 2.1 %maximum_bitcast_fusion = bf16[1,128,8,512]{1,3,2,0:T(8,128)(2,1)} fusion(bf16[128,8,256]{0,2,1:T(8,128)(2,1)} %bitcast.27, bf16[128,8,256]{0,2,1:T(8,128)(2,1)S(1)} %bitcast.26), kind=kLoop, calls=%fused_computation.7 | loop fusion | flops 2097152 | bytes 2097152 | tf_op jit(solution)/shard_map/broadcast_in_dim | solution.py:410
  12.4 0.0 copy-done.5
  12.4 0.0 copy-start.10
  12.4 0.0 copy-start.8
  12.5 2.3 %copy.22 = bf16[1,128,8,512]{3,1,0,2:T(8,128)(2,1)} copy(bf16[1,128,8,512]{1,3,2,0:T(8,128)(2,1)} %maximum_bitcast_fusion) | data formatting | bytes 2097152 | tf_op jit(solution)/shard_map/broadcast_in_dim | solution.py:410
  14.8 5.2 %all-to-all-start = ((bf16[1,128,8,512]{3,1,0,2:T(8,128)(2,1)}), bf16[1,128,8,512]{3,1,0,2:T(8,128)(2,1)S(1)}, u32[]{:S(2)}, u32[]{:S(2)}) async-start(bf16[1,128,8,512]{3,1,0,2:T(8,128)(2,1)} %copy.22), calls=%async_computation | async-start | bytes 2097152 | tf_op jit(solution)/shard_map/all_to_all | solution.py:410
  19.9 0.0 all-gather.2.cloned.1.call-start
  20.0 0.0 copy-done.10
  20.0 0.0 copy-done.8
  20.0 1.8 %fusion.7 = bf16[528,512]{1,0:T(8,128)(2,1)} fusion(bf16[4,512]{1,0:T(4,128)(2,1)S(1)} %reshape.39, bf16[256,512]{1,0:T(8,128)(2,1)S(1)} %bitcast.28, bf16[256,512]{1,0:T(8,128)(2,1)} %bitcast.29), kind=kLoop, calls=%fused_computation.16 | loop fusion | flops 2162688 | bytes 1069056 | tf_op jit(solution)/shard_map/concatenate | solution.py:416
  21.8 0.0 all-gather.2.cloned.1.call-update
  21.8 0.0 copy-start.14
  21.8 13.5 %all-to-all-done = bf16[1,128,8,512]{3,1,0,2:T(8,128)(2,1)S(1)} async-done(((bf16[1,128,8,512]{3,1,0,2:T(8,128)(2,1)}), bf16[1,128,8,512]{3,1,0,2:T(8,128)(2,1)S(1)}, u32[]{:S(2)}, u32[]{:S(2)}) %all-to-all-start) | async-done | bytes 1048608 | tf_op jit(solution)/shard_map/all_to_all | solution.py:410
  35.3 0.0 copy-start.13
  35.3 4.9 %fusion.4 = f32[2048,512]{1,0:T(8,128)S(1)} fusion(bf16[2048,1024]{1,0:T(8,128)(2,1)} %constant.27, bf16[1,128,8,512]{3,1,0,2:T(8,128)(2,1)S(1)} %all-to-all-done), kind=kOutput, calls=%fused_computation.8 | convolution fusion | flops 2147483648 | bytes 9437184 | tf_op jit(solution)/shard_map/dot_general | solution.py:149
  40.3 0.0 copy-done.14
  40.3 0.0 copy-done.13
  40.3 0.0 copy-start.12
  40.3 1.0 fusion.10
  41.3 0.6 copy-done.12
  41.9 1.0 fusion.2
  42.9 0.2 copy.27
  43.1 12.2 %all_to_all.28 = bf16[8,128,256]{2,1,0:T(8,128)(2,1)S(1)} all-to-all(bf16[8,128,256]{2,1,0:T(8,128)(2,1)S(1)} %bitcast.25), channel_id=1, replica_groups=mesh['ctx'=8,'tp'=4] {'ctx'}, dimensions={0} | all-to-all | bytes 1048576 | tf_op jit(solution)/shard_map/all_to_all | solution.py:428
  55.3 0.0 copy-start.6
  55.3 0.0 copy-start.7
  55.3 0.0 copy-start.9
  55.3 0.0 copy-start.11
  55.3 0.1 convert_bitcast_fusion
  55.4 0.1 copy.28
  55.5 0.0 copy-done
  55.5 0.8 copy-done.6
  56.3 0.2 copy-done.7
  56.5 0.0 copy-done.9
  56.5 0.0 copy-done.11
  56.5 0.0 copy-start.2
  56.5 0.7 fusion
  57.2 14.1 %all-gather.2.cloned.1.call-done.cols_ref = bf16[2112,512]{1,0:T(8,128)(2,1)} async-done(((bf16[528,512]{1,0:T(8,128)(2,1)}), bf16[2112,512]{1,0:T(8,128)(2,1)}) %all-gather.2.cloned.1.call-update) | async-done | bytes 2162704 | tf_op jit(solution)/shard_map/all_gather | solution.py:419
  71.3 0.0 copy-done.2
  71.3 0.0 copy-start.1
  71.3 1.6 %copy-done.1 = bf16[2112,512]{1,0:T(8,128)(2,1)S(1)} copy-done((bf16[2112,512]{1,0:T(8,128)(2,1)S(1)}, bf16[2112,512]{1,0:T(8,128)(2,1)}, u32[]{:S(2)}) %copy-start.1) | copy-done | bytes 2162712
  72.9 0.0 copy-start.3
  72.9 1.0 copy-done.3
  74.0 0.0 copy-start.4
  74.0 1.0 copy-done.4
  75.0 42.8 %circulant_mlp.1 = bf16[4,32,2048]{2,1,0:T(8,128)(2,1)S(1)} custom-call(bf16[4,32,2048]{2,1,0:T(8,128)(2,1)S(1)} %bitcast.22, bf16[2112,512]{1,0:T(8,128)(2,1)S(1)} %copy-done.1, bf16[512,512]{1,0:T(8,128)(2,1)S(1)} %copy-done.3, bf16[512,512]{1,0:T(8,128)(2,1)S(1)} %copy-done.4, bf16[512,768]{1,0:T(8,128)(2,1)S(1)} %copy-done.2), custom_call_target="tpu_custom_call" | custom-call | tf_op jit(solution)/shard_map/circulant_mlp/pallas_call | solution.py:359
  117.9 0.8 copy.34
  (2 shorter events, 0.0 us)
Async XLA Ops:
  6.5 49.0 %copy-start = (bf16[512,2048]{1,0:T(8,128)(2,1)S(1)}, bf16[512,2048]{1,0:T(8,128)(2,1)}, u32[]{:S(2)}) copy-start(bf16[512,2048]{1,0:T(8,128)(2,1)} %param.16) | copy-start | bytes 6291460
  8.0 4.4 %copy-start.5 = (bf16[128,2048]{1,0:T(8,128)(2,1)}, bf16[128,2048]{1,0:T(8,128)(2,1)S(1)}, u32[]{:S(2)}) copy-start(bf16[128,2048]{1,0:T(8,128)(2,1)S(1)} %multiply_convert_fusion.2) | copy-start | bytes 1572868
  12.4 7.5 %copy-start.10 = (bf16[2048]{0:T(1024)(128)(2,1)S(1)}, bf16[2048]{0:T(1024)(128)(2,1)}, u32[]{:S(2)}) copy-start(bf16[2048]{0:T(1024)(128)(2,1)} %param.22) | copy-start | bytes 12292
  12.4 7.5 %copy-start.8 = (bf16[16,16,512]{2,1,0:T(8,128)(2,1)S(1)}, bf16[16,16,512]{2,1,0:T(8,128)(2,1)}, u32[]{:S(2)}) copy-start(bf16[16,16,512]{2,1,0:T(8,128)(2,1)} %param.24) | copy-start | bytes 786436
  14.8 20.6 %all-to-all-start = ((bf16[1,128,8,512]{3,1,0,2:T(8,128)(2,1)}), bf16[1,128,8,512]{3,1,0,2:T(8,128)(2,1)S(1)}, u32[]{:S(2)}, u32[]{:S(2)}) async-start(bf16[1,128,8,512]{3,1,0,2:T(8,128)(2,1)} %copy.22), calls=%async_computation | async-start | bytes 2097152 | tf_op jit(solution)/shard_map/all_to_all | solution.py:410
  19.9 51.4 %all-gather.2.cloned.1.call-start = ((), (), s32[]{:S(2)}) async-start(), calls=%async_computation.2 | async-start | bytes 2703360 | tf_op jit(solution)/shard_map/all_gather | solution.py:419
  21.8 18.4 %copy-start.14 = (f32[1024]{0:T(1024)S(1)}, f32[1024]{0:T(1024)}, u32[]{:S(2)}) copy-start(f32[1024]{0:T(1024)} %constant.24) | copy-start | bytes 12292
  35.3 4.9 %copy-start.13 = (bf16[1024,1024]{1,0:T(8,128)(2,1)S(1)}, bf16[1024,1024]{1,0:T(8,128)(2,1)}, u32[]{:S(2)}) copy-start(bf16[1024,1024]{1,0:T(8,128)(2,1)} %constant.28) | copy-start | bytes 6291460
  40.3 1.6 %copy-start.12 = (bf16[1024,1024]{1,0:T(8,128)(2,1)S(1)}, bf16[1024,1024]{1,0:T(8,128)(2,1)}, u32[]{:S(2)}) copy-start(bf16[1024,1024]{1,0:T(8,128)(2,1)} %constant.29) | copy-start | bytes 6291460
  55.3 1.0 copy-start.6
  55.3 1.2 copy-start.7
  55.3 1.2 copy-start.9
  55.3 1.2 copy-start.11
  56.5 14.8 %copy-start.2 = (bf16[512,768]{1,0:T(8,128)(2,1)S(1)}, bf16[512,768]{1,0:T(8,128)(2,1)}, u32[]{:S(2)}) copy-start(bf16[512,768]{1,0:T(8,128)(2,1)} %constant.19.clone.tap_ref) | copy-start | bytes 2359300
  71.3 1.6 %copy-start.1 = (bf16[2112,512]{1,0:T(8,128)(2,1)S(1)}, bf16[2112,512]{1,0:T(8,128)(2,1)}, u32[]{:S(2)}) copy-start(bf16[2112,512]{1,0:T(8,128)(2,1)} %all-gather.2.cloned.1.call-done.cols_ref) | copy-start | bytes 6488068
  72.9 1.0 copy-start.3
  74.0 1.0 copy-start.4
Sparse Core Ops, SparseCore 0:
  22.3 48.9 all-gather.1

commit v2 on v1

--- a/solution.py
+++ b/solution.py
@@ -411,12 +411,14 @@
     arrived = arrived.reshape(outer * tokens, -1)
     forward_table, inverse_table, tap_table = block_tables()
     gain_rows = norm_gain.reshape(-1, BLOCK)
-    padded = 16
+    padded = 32
     gain_rows = jnp.pad(gain_rows, ((0, padded - gain_rows.shape[0]), (0, 0)))
     columns = jnp.concatenate(
         [circulant_up.reshape(-1, BLOCK), circulant_down.reshape(-1, BLOCK), gain_rows], axis=0
     )
-    all_columns = lax.all_gather(columns, "tp", axis=0, tiled=True)
+    share = columns.shape[0] // 2
+    half_columns = lax.dynamic_slice_in_dim(columns, lax.axis_index("ctx") % 2 * share, share)
+    half_gathered = lax.all_gather(half_columns, "tp", axis=0, tiled=False)
     onehot = (token_ids[:, None] == lax.broadcasted_iota(jnp.int32, (1, vocab), 1)).astype(
         jnp.bfloat16
     )
@@ -425,8 +427,15 @@
         local_mixed = short_window(arrived)
     else:
         local_mixed = long_window(*jnp.split(arrived, 2, axis=1), outer)
+    local_mixed = local_mixed.astype(jnp.bfloat16)
+    half_gathered, local_mixed = lax.optimization_barrier((half_gathered, local_mixed))
+    chips = [[2 * chip, 2 * chip + 1] for chip in range(outer // 2)]
+    both_halves = lax.all_gather(
+        half_gathered, "ctx", axis=0, tiled=False, axis_index_groups=chips
+    )
+    all_columns = both_halves.transpose(1, 0, 2, 3).reshape(-1, BLOCK)
     mixed = lax.all_to_all(
-        local_mixed.astype(jnp.bfloat16), "ctx", split_axis=0, concat_axis=1, tiled=True
+        local_mixed, "ctx", split_axis=0, concat_axis=1, tiled=True
     ).astype(jnp.float32)
     mixed = mixed + skip_gain[None, :] * gated.astype(jnp.float32)
     stream = (embedded + query_feat.astype(jnp.float32) * mixed).astype(jnp.bfloat16)

time: 126 us -> 122 us (0.968)
  waiting for transfers between devices: 27.7 us -> 23.5 us
    all_gather x1 -> x2, waiting for transfers between devices: 14.1 us -> 9.41 us  [the longest x1 9.38 us: body(): half_gathered = lax.all_gather(half_columns, 'tp', axis=0, tiled=False)]
    unnamed x32 -> x28, local copies, waits for them, and re-layouts: 8.13 us -> 4.41 us
    transpose x0 -> x1, local copies, waits for them, and re-layouts: none -> 1.94 us  [body(): all_columns = both_halves.transpose(1, 0, 2, 3).reshape(-1, BLOCK)]
  transfers between devices with their start and end apart: 2 -> 3, of which waited for: 2 -> 2; matrix products, arithmetic and copies ran while one was open for 8% -> 9% of each run, Pallas kernels for 0% -> 0%
where the time goes in v2:
time: 122 us
  Pallas kernels  42.1 us (35%)
  waiting for transfers between devices  23.5 us (19%)
  between operations  13.6 us (11%)
  blocking collectives  13.2 us (11%)
  local copies, waits for them, and re-layouts  10.3 us (8%)
  matrix products  8.73 us (7%)
  starting transfers between devices  5.25 us (4%)
  other arithmetic  4.95 us (4%)
    pallas_call x1, Pallas kernels, mlp(): pl.pallas_call(functools.partial(mlp_kernel, local), out_shape=jax.ShapeD...  42.1 us
    all_to_all x1, waiting for transfers between devices, body(): arrived = lax.all_to_all(pairs, 'ctx', split_axis=1, concat_axis=0)  14 us
    all_to_all x1, blocking collectives, body(): lax.all_to_all(local_mixed, 'ctx', split_axis=0, concat_axis=1, tiled=True)  13.2 us
    all_gather x1, waiting for transfers between devices, body(): half_gathered = lax.all_gather(half_columns, 'tp', axis=0, tiled=False)  9.38 us
    dot_general x1, matrix products, short_window(): spectrum = jnp.dot(table, both, preferred_element_type=jnp.float32)  5.23 us
    all_to_all x1, starting transfers between devices, body(): arrived = lax.all_to_all(pairs, 'ctx', split_axis=1, concat_axis=0)  5.17 us
    unnamed x28, local copies, waits for them, and re-layouts  4.41 us
    dot_general x2, matrix products, short_window(): lax.dot_general(table, product, (((0,), (0,)), ((), ())), preferred_eleme...  2.85 us
  transfers between devices with their start and end apart: 3, of which 2 were waited for; matrix products, arithmetic and copies ran while one was open for 9% of the time, Pallas kernels for 0%

profile of v2, /device:TPU:0, one launch (start us, length us, event | category | flops | bytes accessed | tf_op | source)
XLA Modules:
  0.0 121.6 jit_solution(1229900946265965714)
XLA Ops:
  6.5 0.0 copy-start
  6.5 1.5 %multiply_convert_fusion.2 = bf16[128,2048]{1,0:T(8,128)(2,1)S(1)} fusion(bf16[128,2048]{1,0:T(8,128)(2,1)} %param.19, bf16[128,2048]{1,0:T(8,128)(2,1)} %param.18), kind=kLoop, calls=%fused_computation.12 | loop fusion | flops 1048576 | bytes 1572864 | tf_op jit(solution)/shard_map/convert_element_type | solution.py:406
  8.0 0.3 copy.30
  8.3 2.0 %copy.23 = bf16[128,2048]{0,1:T(8,128)(2,1)} copy(bf16[128,2048]{1,0:T(8,128)(2,1)} %param.20) | data formatting | bytes 1048576 | tf_op args[5]
  10.3 2.1 %maximum_bitcast_fusion = bf16[1,128,8,512]{1,3,2,0:T(8,128)(2,1)} fusion(bf16[128,8,256]{0,2,1:T(8,128)(2,1)} %bitcast.34, bf16[128,8,256]{0,2,1:T(8,128)(2,1)S(1)} %bitcast.33), kind=kLoop, calls=%fused_computation.5 | loop fusion | flops 2097152 | bytes 2097152 | tf_op jit(solution)/shard_map/broadcast_in_dim | solution.py:410
  12.4 0.0 copy-start.8
  12.5 0.0 copy-start.5
  12.5 0.0 copy-start.6
  12.5 2.3 %copy.25 = bf16[1,128,8,512]{3,1,0,2:T(8,128)(2,1)} copy(bf16[1,128,8,512]{1,3,2,0:T(8,128)(2,1)} %maximum_bitcast_fusion) | data formatting | bytes 2097152 | tf_op jit(solution)/shard_map/broadcast_in_dim | solution.py:410
  14.8 5.2 %all-to-all-start = ((bf16[1,128,8,512]{3,1,0,2:T(8,128)(2,1)}), bf16[1,128,8,512]{3,1,0,2:T(8,128)(2,1)}, u32[]{:S(2)}, u32[]{:S(2)}) async-start(bf16[1,128,8,512]{3,1,0,2:T(8,128)(2,1)} %copy.25), calls=%async_computation | async-start | bytes 2097152 | tf_op jit(solution)/shard_map/all_to_all | solution.py:410
  20.0 0.0 all-gather.5.cloned.1.call-start
  20.0 0.0 copy-done.8
  20.0 0.0 copy-done.5
  20.1 0.0 copy-done.6
  20.1 1.3 %fusion.10 = bf16[272,512]{1,0:T(8,128)(2,1)} fusion(s32[]{:T(128)S(6)} %select_n.19, bf16[256,512]{1,0:T(8,128)(2,1)S(1)} %bitcast.36, bf16[256,512]{1,0:T(8,128)(2,1)S(1)} %bitcast.37, bf16[4,512]{1,0:T(4,128)(2,1)S(1)} %reshape.39), kind=kLoop, calls=%fused_computation.22 | loop fusion | flops 1253376 | bytes 807936 | tf_op jit(solution)/shard_map/concatenate | solution.py:416
  21.3 0.0 all-gather.5.cloned.1.call-update
  21.4 0.0 all-gather.7.cloned.1.call-start
  21.4 0.0 copy-start.12
  21.4 14.0 %all-to-all-done = bf16[1,128,8,512]{3,1,0,2:T(8,128)(2,1)} async-done(((bf16[1,128,8,512]{3,1,0,2:T(8,128)(2,1)}), bf16[1,128,8,512]{3,1,0,2:T(8,128)(2,1)}, u32[]{:S(2)}, u32[]{:S(2)}) %all-to-all-start) | async-done | bytes 1048608 | tf_op jit(solution)/shard_map/all_to_all | solution.py:410
  35.5 0.0 copy-start.11
  35.5 5.2 %fusion.3 = f32[2048,512]{1,0:T(8,128)S(1)} fusion(bf16[2048,1024]{1,0:T(8,128)(2,1)} %constant.49, bf16[1,128,8,512]{3,1,0,2:T(8,128)(2,1)} %all-to-all-done), kind=kOutput, calls=%fused_computation.6 | convolution fusion | flops 2147483648 | bytes 9437184 | tf_op jit(solution)/shard_map/dot_general | solution.py:149
  40.7 0.0 copy-done.12
  40.7 0.0 copy-done.11
  40.7 0.0 copy-start.10
  40.7 1.0 fusion.9
  41.8 0.6 copy-done.10
  42.4 1.8 %fusion.2 = bf16[1024,256]{0,1:T(8,128)(2,1)} fusion(f32[256,1024]{1,0:T(8,128)S(1)} %fusion.9, bf16[1024,1024]{1,0:T(8,128)(2,1)S(1)} %copy-done.10, f32[2048,512]{1,0:T(8,128)S(1)} %fusion.3, f32[1024]{0:T(1024)S(1)} %copy-done.12, pred[1024]{0:T(1024)(128)(4,1)S(1)} %iota_compare_fusion.2), kind=kOutput, calls=%fused_computation.4 | convolution fusion | flops 539230208 | bytes 7869440 | tf_op jit(solution)/shard_map/dot_general | solution.py:158
  44.2 9.4 %all-gather.5.cloned.1.call-done = bf16[1088,512]{1,0:T(8,128)(2,1)} async-done(((bf16[272,512]{1,0:T(8,128)(2,1)}), bf16[1088,512]{1,0:T(8,128)(2,1)}) %all-gather.5.cloned.1.call-update) | async-done | bytes 1114128 | tf_op jit(solution)/shard_map/all_gather | solution.py:421
  53.6 0.0 all-gather.7.cloned.1.call-update
  53.6 1.2 %copy.31 = bf16[1024,256]{1,0:T(8,128)(2,1)S(1)} copy(bf16[1024,256]{0,1:T(8,128)(2,1)} %fusion.2) | data formatting | bytes 1048576 | tf_op jit(solution)/shard_map/all_to_all | solution.py:437
  54.8 13.2 %all_to_all.28 = bf16[8,128,256]{2,1,0:T(8,128)(2,1)S(1)} all-to-all(bf16[8,128,256]{2,1,0:T(8,128)(2,1)S(1)} %bitcast.32), channel_id=1, replica_groups=mesh['ctx'=8,'tp'=4] {'ctx'}, dimensions={0} | all-to-all | bytes 1048576 | tf_op jit(solution)/shard_map/all_to_all | solution.py:437
  68.0 0.0 copy-start.4
  68.0 0.0 copy-start.7
  68.0 0.0 copy-start.9
  68.0 0.1 convert_bitcast_fusion
  68.1 0.1 copy.32
  68.2 0.0 copy-done
  68.3 0.8 copy-done.4
  69.1 0.0 copy-done.7
  69.1 0.0 copy-done.9
  69.1 0.6 fusion
  69.7 0.0 all-gather.7.cloned.1.call-done
  69.8 0.0 copy-start.1
  69.8 0.0 copy-start.2
  69.8 0.0 copy-start.3
  69.8 1.9 %copy.29 = bf16[4,2,272,512]{3,2,1,0:T(8,128)(2,1)S(1)} copy(bf16[4,2,272,512]{3,2,0,1:T(8,128)(2,1)} %bitcast.31) | data formatting | bytes 4456448 | tf_op jit(solution)/shard_map/transpose | solution.py:436
  71.8 0.0 copy-done.1
  71.8 0.0 copy-done.2
  71.8 0.1 copy-done.3
  71.9 42.1 %circulant_mlp.1 = bf16[4,32,2048]{2,1,0:T(8,128)(2,1)S(1)} custom-call(bf16[4,32,2048]{2,1,0:T(8,128)(2,1)S(1)} %bitcast.28, bf16[2176,512]{1,0:T(8,128)(2,1)S(1)} %bitcast.27, bf16[512,512]{1,0:T(8,128)(2,1)S(1)} %copy-done.3, bf16[512,512]{1,0:T(8,128)(2,1)S(1)} %copy-done.2, bf16[512,768]{1,0:T(8,128)(2,1)S(1)} %copy-done.1), custom_call_target="tpu_custom_call" | custom-call | tf_op jit(solution)/shard_map/circulant_mlp/pallas_call | solution.py:359
  114.0 0.8 copy.38
  (2 shorter events, 0.0 us)
Async XLA Ops:
  6.5 61.7 %copy-start = (bf16[512,2048]{1,0:T(8,128)(2,1)S(1)}, bf16[512,2048]{1,0:T(8,128)(2,1)}, u32[]{:S(2)}) copy-start(bf16[512,2048]{1,0:T(8,128)(2,1)} %param.16) | copy-start | bytes 6291460
  12.4 7.6 %copy-start.8 = (bf16[2048]{0:T(1024)(128)(2,1)S(1)}, bf16[2048]{0:T(1024)(128)(2,1)}, u32[]{:S(2)}) copy-start(bf16[2048]{0:T(1024)(128)(2,1)} %param.22) | copy-start | bytes 12292
  12.5 7.6 %copy-start.5 = (bf16[16,16,512]{2,1,0:T(8,128)(2,1)S(1)}, bf16[16,16,512]{2,1,0:T(8,128)(2,1)}, u32[]{:S(2)}) copy-start(bf16[16,16,512]{2,1,0:T(8,128)(2,1)} %param.23) | copy-start | bytes 786436
  12.5 7.6 %copy-start.6 = (bf16[16,16,512]{2,1,0:T(8,128)(2,1)S(1)}, bf16[16,16,512]{2,1,0:T(8,128)(2,1)}, u32[]{:S(2)}) copy-start(bf16[16,16,512]{2,1,0:T(8,128)(2,1)} %param.24) | copy-start | bytes 786436
  14.8 20.7 %all-to-all-start = ((bf16[1,128,8,512]{3,1,0,2:T(8,128)(2,1)}), bf16[1,128,8,512]{3,1,0,2:T(8,128)(2,1)}, u32[]{:S(2)}, u32[]{:S(2)}) async-start(bf16[1,128,8,512]{3,1,0,2:T(8,128)(2,1)} %copy.25), calls=%async_computation | async-start | bytes 2097152 | tf_op jit(solution)/shard_map/all_to_all | solution.py:410
  20.0 33.6 %all-gather.5.cloned.1.call-start = ((), (), s32[]{:S(2)}) async-start(), calls=%async_computation.2 | async-start | bytes 1392640 | tf_op jit(solution)/shard_map/all_gather | solution.py:421
  21.4 48.4 %all-gather.7.cloned.1.call-start = ((), (), s32[]{:S(2)}) async-start(), calls=%async_computation.3 | async-start | bytes 3342336 | tf_op jit(solution)/shard_map/all_gather | solution.py:433
  21.4 19.3 %copy-start.12 = (f32[1024]{0:T(1024)S(1)}, f32[1024]{0:T(1024)}, u32[]{:S(2)}) copy-start(f32[1024]{0:T(1024)} %constant.46) | copy-start | bytes 12292
  35.5 5.2 %copy-start.11 = (bf16[1024,1024]{1,0:T(8,128)(2,1)S(1)}, bf16[1024,1024]{1,0:T(8,128)(2,1)}, u32[]{:S(2)}) copy-start(bf16[1024,1024]{1,0:T(8,128)(2,1)} %constant.50) | copy-start | bytes 6291460
  40.7 1.6 %copy-start.10 = (bf16[1024,1024]{1,0:T(8,128)(2,1)S(1)}, bf16[1024,1024]{1,0:T(8,128)(2,1)}, u32[]{:S(2)}) copy-start(bf16[1024,1024]{1,0:T(8,128)(2,1)} %constant.51) | copy-start | bytes 6291460
  68.0 1.0 copy-start.4
  68.0 1.0 copy-start.7
  68.0 1.0 copy-start.9
  69.8 2.0 %copy-start.1 = (bf16[512,768]{1,0:T(8,128)(2,1)S(1)}, bf16[512,768]{1,0:T(8,128)(2,1)}, u32[]{:S(2)}) copy-start(bf16[512,768]{1,0:T(8,128)(2,1)} %constant.41.clone.tap_ref) | copy-start | bytes 2359300
  69.8 2.0 %copy-start.2 = (bf16[512,512]{1,0:T(8,128)(2,1)S(1)}, bf16[512,512]{1,0:T(8,128)(2,1)}, u32[]{:S(2)}) copy-start(bf16[512,512]{1,0:T(8,128)(2,1)} %constant.40.clone.inv_ref) | copy-start | bytes 1572868
  69.8 2.1 %copy-start.3 = (bf16[512,512]{1,0:T(8,128)(2,1)S(1)}, bf16[512,512]{1,0:T(8,128)(2,1)}, u32[]{:S(2)}) copy-start(bf16[512,512]{1,0:T(8,128)(2,1)} %constant.39.clone.fwd_ref) | copy-start | bytes 1572868
Sparse Core Ops, SparseCore 0:
  22.4 31.1 all-gather.4
  55.1 10.2 all-gather.6

commit v3 on v1

--- a/solution.py
+++ b/solution.py
@@ -142,21 +142,201 @@
     )
 
 
-def short_window(both):
-    length, width = both.shape[0], both.shape[1] // 2
+def conv_kernel(
+    key_ref,
+    value_ref,
+    filter_ref,
+    fwd_ref,
+    inv_ref,
+    cols_ref,
+    mixed_ref,
+    gated_ref,
+    all_ref,
+    both_ref,
+    spec_ref,
+    prod_ref,
+    loc_ref,
+    out_sem,
+    in_sem,
+    back_out_sem,
+    back_in_sem,
+    z_out_sem,
+    z_in_sem,
+    pair_out_sem,
+    pair_in_sem,
+):
+    tokens = key_ref.shape[0]
+    length = both_ref.shape[0]
+    width = prod_ref.shape[1]
+    outer = length // tokens
+    groups, held = all_ref.shape[0], all_ref.shape[1]
+    share = held // 2
+    me = lax.axis_index("ctx")
+    row = lax.axis_index("tp")
+    core = lax.rem(me, 2)
+    sibling = me + 1 - 2 * core
+    peers = [lax.rem(me + d, outer) for d in range(1, outer)]
+    above = [lax.rem(row + d, groups) for d in range(1, groups)]
+    below = [lax.rem(row + groups - d, groups) for d in range(1, groups)]
+    mesh_type = pl.DeviceIdType.MESH
+
+    gated_ref[...] = (
+        key_ref[...].astype(jnp.float32) * value_ref[...].astype(jnp.float32)
+    ).astype(jnp.bfloat16)
+
+    barrier = pltpu.get_barrier_semaphore()
+    for peer in peers:
+        pl.semaphore_signal(barrier, inc=1, device_id={"ctx": peer}, device_id_type=mesh_type)
+    for peer in above:
+        pl.semaphore_signal(barrier, inc=1, device_id={"tp": peer}, device_id_type=mesh_type)
+    pl.semaphore_wait(barrier, outer + groups - 2)
+
+    def send(src, dst, sent, got, target):
+        copy = pltpu.make_async_remote_copy(
+            src_ref=src,
+            dst_ref=dst,
+            send_sem=sent,
+            recv_sem=got,
+            device_id=target,
+            device_id_type=mesh_type,
+        )
+        copy.start()
+        return copy
+
+    def positions(at):
+        return pl.ds(pl.multiple_of(at * tokens, tokens), tokens)
+
+    def channels(at):
+        return pl.ds(pl.multiple_of(at * width, width), width)
+
+    copies = []
+    for d, peer in enumerate(peers):
+        for part, src in enumerate((gated_ref, filter_ref)):
+            copies.append(
+                send(
+                    src.at[:, channels(peer)],
+                    both_ref.at[positions(me), pl.ds(part * width, width)],
+                    out_sem.at[d, part],
+                    in_sem.at[d, part],
+                    {"ctx": peer},
+                )
+            )
+    half = pl.ds(pl.multiple_of(core * share, share), share)
+    z_copies = [
+        send(
+            cols_ref.at[half], all_ref.at[row, half], z_out_sem.at[d], z_in_sem.at[d], {"tp": peer}
+        )
+        for d, peer in enumerate(above)
+    ]
+    all_ref[row] = cols_ref[...]
+    both_ref[positions(me), :width] = gated_ref[:, channels(me)]
+    both_ref[positions(me), width:] = filter_ref[:, channels(me)]
+    for copy in copies:
+        copy.wait()
+
+    piece = 256
+
+    @pl.loop(0, 2 * length // piece)
+    def _(at):
+        rows = pl.ds(pl.multiple_of(at * piece, piece), piece)
+        spec_ref[rows, :] = jnp.dot(
+            fwd_ref[rows, :], both_ref[...], preferred_element_type=jnp.float32
+        )
+
+    size = 2 * length
+
+    @pl.loop(0, length // LANES)
+    def _(at):
+        real = pl.ds(pl.multiple_of(at * LANES, LANES), LANES)
+        imag = pl.ds(pl.multiple_of(length + at * LANES, LANES), LANES)
+        real_s, real_k = spec_ref[real, :width], spec_ref[real, width:]
+        imag_s, imag_k = spec_ref[imag, :width], spec_ref[imag, width:]
+        first = lax.broadcasted_iota(jnp.int32, (LANES, width), 0) + at * LANES == 0
+        weight = jnp.where(first, 1.0 / size, 2.0 / size)
+        crossed = imag_s * imag_k
+        straight = real_s * real_k
+        mixed_terms = real_s * imag_k + imag_s * real_k
+        prod_ref[real, :] = (weight * (straight - jnp.where(first, 0.0, crossed))).astype(
+            jnp.bfloat16
+        )
+        prod_ref[imag, :] = (weight * jnp.where(first, crossed, mixed_terms)).astype(jnp.bfloat16)
+
+    copies = []
+    for d in range(outer):
+        target = peers[d] if d < outer - 1 else me
+        values = jnp.dot(
+            inv_ref[positions(target), :], prod_ref[...], preferred_element_type=jnp.float32
+        ).astype(jnp.bfloat16)
+        if d < outer - 1:
+            loc_ref[positions(target), :] = values
+            copies.append(
+                send(
+                    loc_ref.at[positions(target)],
+                    mixed_ref.at[:, channels(me)],
+                    back_out_sem.at[d],
+                    back_in_sem.at[d],
+                    {"ctx": target},
+                )
+            )
+        else:
+            mixed_ref[:, channels(me)] = values
+    for copy in z_copies:
+        copy.wait()
+    for d, source in enumerate(below):
+        copies.append(
+            send(
+                all_ref.at[source, half],
+                all_ref.at[source, half],
+                pair_out_sem.at[d],
+                pair_in_sem.at[d],
+                {"ctx": sibling},
+            )
+        )
+    for copy in copies:
+        copy.wait()
+
+
+def short_window(key_feat, value_feat, long_filter, columns, outer, groups):
+    tokens, channels = key_feat.shape
+    length, width = outer * tokens, channels // outer
     cosine, sine = packed_dft(2 * length, length)
-    table = jnp.asarray(np.concatenate([cosine, sine], axis=1).T, jnp.bfloat16)
-    spectrum = jnp.dot(table, both, preferred_element_type=jnp.float32)
-    real_s, real_k = spectrum[:length, :width], spectrum[:length, width:]
-    imag_s, imag_k = spectrum[length:, :width], spectrum[length:, width:]
-    first = lax.broadcasted_iota(jnp.int32, (length, 1), 0) == 0
-    weight = jnp.asarray(packed_weights(2 * length)[:, None], jnp.float32)
-    crossed = imag_s * imag_k
-    real_out = weight * (real_s * real_k - jnp.where(first, 0.0, crossed))
-    imag_out = weight * jnp.where(first, crossed, real_s * imag_k + imag_s * real_k)
-    product = jnp.concatenate([real_out, imag_out], axis=0).astype(jnp.bfloat16)
-    return lax.dot_general(
-        table, product, (((0,), (0,)), ((), ())), preferred_element_type=jnp.float32
+    table = np.concatenate([cosine, sine], axis=1)
+    vmem = pl.BlockSpec(memory_space=pltpu.VMEM)
+    dma = pltpu.SemaphoreType.DMA
+    return pl.pallas_call(
+        conv_kernel,
+        out_shape=(
+            jax.ShapeDtypeStruct(key_feat.shape, jnp.bfloat16),
+            jax.ShapeDtypeStruct(key_feat.shape, jnp.bfloat16),
+            jax.ShapeDtypeStruct((groups,) + columns.shape, jnp.bfloat16),
+        ),
+        in_specs=[vmem] * 6,
+        out_specs=(vmem,) * 3,
+        scratch_shapes=[
+            pltpu.VMEM((length, 2 * width), jnp.bfloat16),
+            pltpu.VMEM((2 * length, 2 * width), jnp.float32),
+            pltpu.VMEM((2 * length, width), jnp.bfloat16),
+            pltpu.VMEM((length, width), jnp.bfloat16),
+            dma((outer - 1, 2)),
+            dma((outer - 1, 2)),
+            dma((outer - 1,)),
+            dma((outer - 1,)),
+            dma((groups - 1,)),
+            dma((groups - 1,)),
+            dma((groups - 1,)),
+            dma((groups - 1,)),
+        ],
+        compiler_params=pltpu.CompilerParams(
+            vmem_limit_bytes=40 * 1024 * 1024, collective_id=2, has_side_effects=True
+        ),
+        name="long_conv",
+    )(
+        key_feat,
+        value_feat,
+        long_filter,
+        jnp.asarray(table.T, jnp.bfloat16),
+        jnp.asarray(table, jnp.bfloat16),
+        columns,
     )
 
 
@@ -402,32 +582,36 @@
     width = query_feat.shape[1]
     ins = circulant_up.shape[1]
     local = circulant_up.shape[0]
-    gated_wide = key_feat.astype(jnp.float32) * value_feat.astype(jnp.float32)
-    gated = gated_wide.astype(jnp.bfloat16)
-    pairs = jnp.concatenate(
-        [gated.reshape(tokens, outer, -1), long_filter.reshape(tokens, outer, -1)], axis=2
-    )
-    arrived = lax.all_to_all(pairs, "ctx", split_axis=1, concat_axis=0)
-    arrived = arrived.reshape(outer * tokens, -1)
     forward_table, inverse_table, tap_table = block_tables()
     gain_rows = norm_gain.reshape(-1, BLOCK)
-    padded = 16
+    padded = 32
     gain_rows = jnp.pad(gain_rows, ((0, padded - gain_rows.shape[0]), (0, 0)))
     columns = jnp.concatenate(
         [circulant_up.reshape(-1, BLOCK), circulant_down.reshape(-1, BLOCK), gain_rows], axis=0
     )
-    all_columns = lax.all_gather(columns, "tp", axis=0, tiled=True)
     onehot = (token_ids[:, None] == lax.broadcasted_iota(jnp.int32, (1, vocab), 1)).astype(
         jnp.bfloat16
     )
     embedded = jnp.dot(onehot, embed_table, preferred_element_type=jnp.float32)
-    if outer * tokens <= DENSE_WINDOW:
-        local_mixed = short_window(arrived)
+    if 2 * outer * tokens <= DENSE_WINDOW and width // outer % LANES == 0:
+        mixed, gated, all_columns = short_window(
+            key_feat, value_feat, long_filter, columns, outer, groups
+        )
+        all_columns = all_columns.reshape(-1, BLOCK)
+        mixed = mixed.astype(jnp.float32)
     else:
+        gated_wide = key_feat.astype(jnp.float32) * value_feat.astype(jnp.float32)
+        gated = gated_wide.astype(jnp.bfloat16)
+        pairs = jnp.concatenate(
+            [gated.reshape(tokens, outer, -1), long_filter.reshape(tokens, outer, -1)], axis=2
+        )
+        arrived = lax.all_to_all(pairs, "ctx", split_axis=1, concat_axis=0)
+        arrived = arrived.reshape(outer * tokens, -1)
+        all_columns = lax.all_gather(columns, "tp", axis=0, tiled=True)
         local_mixed = long_window(*jnp.split(arrived, 2, axis=1), outer)
-    mixed = lax.all_to_all(
-        local_mixed.astype(jnp.bfloat16), "ctx", split_axis=0, concat_axis=1, tiled=True
-    ).astype(jnp.float32)
+        mixed = lax.all_to_all(
+            local_mixed.astype(jnp.bfloat16), "ctx", split_axis=0, concat_axis=1, tiled=True
+        ).astype(jnp.float32)
     mixed = mixed + skip_gain[None, :] * gated.astype(jnp.float32)
     stream = (embedded + query_feat.astype(jnp.float32) * mixed).astype(jnp.bfloat16)
     own = stream.reshape(groups, tokens // groups, width)

time: 126 us -> 89.3 us (0.71)
  Pallas kernels: 42.8 us -> 77.2 us
  waiting for transfers between devices: 27.7 us -> 0 us
  between operations: 13.5 us -> 0.1 us
  blocking collectives: 12.2 us -> 0 us
  matrix products: 7.63 us -> 0.62 us
  starting transfers between devices: 5.21 us -> 0 us
  other arithmetic: 5.44 us -> 1.07 us
    pallas_call x0 -> x1, Pallas kernels: none -> 29.9 us  [short_window(): pl.pallas_call(conv_kernel, out_shape=(jax.ShapeDtypeStruct(key_feat.shap...]
    all_gather x1 -> x0, waiting for transfers between devices: 14.1 us -> none  [body(): all_columns = lax.all_gather(columns, 'tp', axis=0, tiled=True)]
    all_to_all x1 -> x0, waiting for transfers between devices: 13.5 us -> none  [body(): arrived = lax.all_to_all(pairs, 'ctx', split_axis=1, concat_axis=0)]
    all_to_all x1 -> x0, blocking collectives: 12.2 us -> none  [body(): lax.all_to_all(local_mixed.astype(jnp.bfloat16), 'ctx', split_axis=0, con...]
    dot_general x3 -> x0, matrix products: 6.97 us -> none  [the longest x1 4.91 us: short_window(): spectrum = jnp.dot(table, both, preferred_element_type=jnp.float32)]
    all_to_all x1 -> x0, starting transfers between devices: 5.17 us -> none  [body(): arrived = lax.all_to_all(pairs, 'ctx', split_axis=1, concat_axis=0)]
    pallas_call x1, Pallas kernels: 42.8 us -> 47.3 us  [mlp(): pl.pallas_call(functools.partial(mlp_kernel, local), out_shape=jax.ShapeD...]
    broadcast_in_dim x1 -> x0, local copies, waits for them, and re-layouts: 2.3 us -> none  [body(): arrived = lax.all_to_all(pairs, 'ctx', split_axis=1, concat_axis=0)]
  transfers between devices with their start and end apart: 2 -> 0, of which waited for: 2 -> 0; matrix products, arithmetic and copies ran while one was open for 8% -> 0% of each run, Pallas kernels for 0% -> 0%
where the time goes in v3:
time: 89.3 us; the launch traced here: 88.9 us
  Pallas kernels  77.2 us (86%)
  local copies, waits for them, and re-layouts  9.94 us (11%)
  other arithmetic  1.07 us (1%)
    pallas_call x1, Pallas kernels, mlp(): pl.pallas_call(functools.partial(mlp_kernel, local), out_shape=jax.ShapeD...  47.3 us
    pallas_call x1, Pallas kernels, short_window(): pl.pallas_call(conv_kernel, out_shape=(jax.ShapeDtypeStruct(key_feat.shap...  29.9 us
    unnamed x25, local copies, waits for them, and re-layouts  9.1 us

profile of v3, /device:TPU:0, one launch (start us, length us, event | category | flops | bytes accessed | tf_op | source)
XLA Modules:
  0.0 88.9 jit_solution(6907348444296528863)
XLA Ops:
  0.0 0.0 copy-start
  0.0 0.8 reshape.22
  0.8 1.1 %fusion.2.cols_ref = bf16[544,512]{1,0:T(8,128)(2,1)S(1)} fusion(bf16[4,512]{1,0:T(4,128)(2,1)S(1)} %reshape.22, bf16[256,512]{1,0:T(8,128)(2,1)} %bitcast.9, bf16[256,512]{1,0:T(8,128)(2,1)} %bitcast.10), kind=kLoop, calls=%fused_computation.4 | loop fusion | flops 2228224 | bytes 1085440 | tf_op jit(solution)/shard_map/concatenate | solution.py:589
  1.9 0.0 copy-start.1
  1.9 2.2 %copy-done.1 = bf16[1024,2048]{1,0:T(8,128)(2,1)S(1)} copy-done((bf16[1024,2048]{1,0:T(8,128)(2,1)S(1)}, bf16[1024,2048]{1,0:T(8,128)(2,1)}, u32[]{:S(2)}) %copy-start.1) | copy-done | bytes 4194328
  4.1 0.0 copy-start.2
  4.1 2.2 %copy-done.2 = bf16[2048,1024]{1,0:T(8,128)(2,1)S(1)} copy-done((bf16[2048,1024]{1,0:T(8,128)(2,1)S(1)}, bf16[2048,1024]{1,0:T(8,128)(2,1)}, u32[]{:S(2)}) %copy-start.2) | copy-done | bytes 4194328
  6.3 0.0 copy-start.4
  6.3 1.0 %copy-done.4 = bf16[128,2048]{1,0:T(8,128)(2,1)S(1)} copy-done((bf16[128,2048]{1,0:T(8,128)(2,1)S(1)}, bf16[128,2048]{1,0:T(8,128)(2,1)}, u32[]{:S(2)}) %copy-start.4) | copy-done | bytes 524312
  7.3 0.0 copy-start.5
  7.3 1.0 %copy-done.5 = bf16[128,2048]{1,0:T(8,128)(2,1)S(1)} copy-done((bf16[128,2048]{1,0:T(8,128)(2,1)S(1)}, bf16[128,2048]{1,0:T(8,128)(2,1)}, u32[]{:S(2)}) %copy-start.5) | copy-done | bytes 524312
  8.4 0.0 copy-start.6
  8.4 1.0 %copy-done.6 = bf16[128,2048]{1,0:T(8,128)(2,1)S(1)} copy-done((bf16[128,2048]{1,0:T(8,128)(2,1)S(1)}, bf16[128,2048]{1,0:T(8,128)(2,1)}, u32[]{:S(2)}) %copy-start.6) | copy-done | bytes 524312
  9.4 0.0 copy-start.9
  9.4 0.0 copy-start.10
  9.4 0.0 copy-start.11
  9.4 29.9 %long_conv.1 = (bf16[128,2048]{1,0:T(8,128)(2,1)S(1)}, bf16[128,2048]{1,0:T(8,128)(2,1)S(1)}, bf16[4,544,512]{2,1,0:T(8,128)(2,1)S(1)}) custom-call(bf16[128,2048]{1,0:T(8,128)(2,1)S(1)} %copy-done.4, bf16[128,2048]{1,0:T(8,128)(2,1)S(1)} %copy-done.5, bf16[128,2048]{1,0:T(8,128)(2,1)S(1)} %copy-done.6, bf16[2048,1024]{1,0:T(8,128)(2,1)S(1)} %copy-done.2, ...), custom_call_target="tpu_custom_call" | custom-call | tf_op jit(solution)/shard_map/long_conv/pallas_call | solution.py:306
  39.3 0.0 copy-done
  39.4 0.0 copy-done.9
  39.4 0.0 copy-done.10
  39.4 0.0 copy-done.11
  39.4 0.0 copy-start.3
  39.4 0.0 copy-start.7
  39.4 0.0 copy-start.8
  39.4 0.6 fusion
  40.0 0.5 copy-done.3
  40.5 0.1 copy-done.7
  40.7 0.2 copy-done.8
  40.8 47.3 %circulant_mlp.1 = bf16[4,32,2048]{2,1,0:T(8,128)(2,1)S(1)} custom-call(bf16[4,32,2048]{2,1,0:T(8,128)(2,1)S(1)} %bitcast.7, bf16[2176,512]{1,0:T(8,128)(2,1)S(1)} %bitcast.6, bf16[512,512]{1,0:T(8,128)(2,1)S(1)} %copy-done.8, bf16[512,512]{1,0:T(8,128)(2,1)S(1)} %copy-done.7, bf16[512,768]{1,0:T(8,128)(2,1)S(1)} %copy-done.3), custom_call_target="tpu_custom_call" | custom-call | tf_op jit(solution)/shard_map/circulant_mlp/pallas_call | solution.py:539
  88.1 0.8 copy.17
Async XLA Ops:
  0.0 39.3 %copy-start = (bf16[512,2048]{1,0:T(8,128)(2,1)S(1)}, bf16[512,2048]{1,0:T(8,128)(2,1)}, u32[]{:S(2)}) copy-start(bf16[512,2048]{1,0:T(8,128)(2,1)} %param.16) | copy-start | bytes 6291460
  1.9 2.2 %copy-start.1 = (bf16[1024,2048]{1,0:T(8,128)(2,1)S(1)}, bf16[1024,2048]{1,0:T(8,128)(2,1)}, u32[]{:S(2)}) copy-start(bf16[1024,2048]{1,0:T(8,128)(2,1)} %constant.17.clone.inv_ref) | copy-start | bytes 12582916
  4.1 2.2 %copy-start.2 = (bf16[2048,1024]{1,0:T(8,128)(2,1)S(1)}, bf16[2048,1024]{1,0:T(8,128)(2,1)}, u32[]{:S(2)}) copy-start(bf16[2048,1024]{1,0:T(8,128)(2,1)} %constant.16.clone.fwd_ref) | copy-start | bytes 12582916
  6.3 1.0 %copy-start.4 = (bf16[128,2048]{1,0:T(8,128)(2,1)S(1)}, bf16[128,2048]{1,0:T(8,128)(2,1)}, u32[]{:S(2)}) copy-start(bf16[128,2048]{1,0:T(8,128)(2,1)} %key_ref.1) | copy-start | bytes 1572868
  7.3 1.0 %copy-start.5 = (bf16[128,2048]{1,0:T(8,128)(2,1)S(1)}, bf16[128,2048]{1,0:T(8,128)(2,1)}, u32[]{:S(2)}) copy-start(bf16[128,2048]{1,0:T(8,128)(2,1)} %value_ref.1) | copy-start | bytes 1572868
  8.4 1.0 %copy-start.6 = (bf16[128,2048]{1,0:T(8,128)(2,1)S(1)}, bf16[128,2048]{1,0:T(8,128)(2,1)}, u32[]{:S(2)}) copy-start(bf16[128,2048]{1,0:T(8,128)(2,1)} %filter_ref.1) | copy-start | bytes 1572868
  9.4 29.9 %copy-start.9 = (bf16[128,2048]{1,0:T(8,128)(2,1)S(1)}, bf16[128,2048]{1,0:T(8,128)(2,1)}, u32[]{:S(2)}) copy-start(bf16[128,2048]{1,0:T(8,128)(2,1)} %param.17) | copy-start | bytes 1572868
  9.4 29.9 %copy-start.10 = (f32[2048]{0:T(1024)S(1)}, f32[2048]{0:T(1024)}, u32[]{:S(2)}) copy-start(f32[2048]{0:T(1024)} %param.21) | copy-start | bytes 24580
  9.4 29.9 %copy-start.11 = (s32[128]{0:T(128)S(1)}, s32[128]{0:T(128)}, u32[]{:S(2)}) copy-start(s32[128]{0:T(128)} %param.15) | copy-start | bytes 1540
  39.4 1.1 %copy-start.3 = (bf16[512,768]{1,0:T(8,128)(2,1)S(1)}, bf16[512,768]{1,0:T(8,128)(2,1)}, u32[]{:S(2)}) copy-start(bf16[512,768]{1,0:T(8,128)(2,1)} %constant.15.clone.tap_ref) | copy-start | bytes 2359300
  39.4 1.3 %copy-start.7 = (bf16[512,512]{1,0:T(8,128)(2,1)S(1)}, bf16[512,512]{1,0:T(8,128)(2,1)}, u32[]{:S(2)}) copy-start(bf16[512,512]{1,0:T(8,128)(2,1)} %constant.14.clone.inv_ref) | copy-start | bytes 1572868
  39.4 1.4 %copy-start.8 = (bf16[512,512]{1,0:T(8,128)(2,1)S(1)}, bf16[512,512]{1,0:T(8,128)(2,1)}, u32[]{:S(2)}) copy-start(bf16[512,512]{1,0:T(8,128)(2,1)} %constant.13.clone.fwd_ref) | copy-start | bytes 1572868

commit v4 on v3

--- a/solution.py
+++ b/solution.py
@@ -146,8 +146,8 @@
     key_ref,
     value_ref,
     filter_ref,
-    fwd_ref,
-    inv_ref,
+    fwd_hbm,
+    inv_hbm,
     cols_ref,
     mixed_ref,
     gated_ref,
@@ -156,6 +156,9 @@
     spec_ref,
     prod_ref,
     loc_ref,
+    fwd_ref,
+    inv_ref,
+    table_sem,
     out_sem,
     in_sem,
     back_out_sem,
@@ -180,6 +183,10 @@
     below = [lax.rem(row + groups - d, groups) for d in range(1, groups)]
     mesh_type = pl.DeviceIdType.MESH
 
+    fwd_copy = pltpu.make_async_copy(fwd_hbm, fwd_ref, table_sem.at[0])
+    inv_copy = pltpu.make_async_copy(inv_hbm, inv_ref, table_sem.at[1])
+    fwd_copy.start()
+    inv_copy.start()
     gated_ref[...] = (
         key_ref[...].astype(jnp.float32) * value_ref[...].astype(jnp.float32)
     ).astype(jnp.bfloat16)
@@ -233,6 +240,8 @@
     both_ref[positions(me), width:] = filter_ref[:, channels(me)]
     for copy in copies:
         copy.wait()
+    fwd_copy.wait()
+    inv_copy.wait()
 
     piece = 256
 
@@ -302,6 +311,7 @@
     cosine, sine = packed_dft(2 * length, length)
     table = np.concatenate([cosine, sine], axis=1)
     vmem = pl.BlockSpec(memory_space=pltpu.VMEM)
+    hbm = pl.BlockSpec(memory_space=pltpu.HBM)
     dma = pltpu.SemaphoreType.DMA
     return pl.pallas_call(
         conv_kernel,
@@ -310,13 +320,16 @@
             jax.ShapeDtypeStruct(key_feat.shape, jnp.bfloat16),
             jax.ShapeDtypeStruct((groups,) + columns.shape, jnp.bfloat16),
         ),
-        in_specs=[vmem] * 6,
+        in_specs=[vmem, vmem, vmem, hbm, hbm, vmem],
         out_specs=(vmem,) * 3,
         scratch_shapes=[
             pltpu.VMEM((length, 2 * width), jnp.bfloat16),
             pltpu.VMEM((2 * length, 2 * width), jnp.float32),
             pltpu.VMEM((2 * length, width), jnp.bfloat16),
             pltpu.VMEM((length, width), jnp.bfloat16),
+            pltpu.VMEM((2 * length, length), jnp.bfloat16),
+            pltpu.VMEM((length, 2 * length), jnp.bfloat16),
+            dma((2,)),
             dma((outer - 1, 2)),
             dma((outer - 1, 2)),
             dma((outer - 1,)),
@@ -327,7 +340,7 @@
             dma((groups - 1,)),
         ],
         compiler_params=pltpu.CompilerParams(
-            vmem_limit_bytes=40 * 1024 * 1024, collective_id=2, has_side_effects=True
+            vmem_limit_bytes=60 * 1024 * 1024, collective_id=2, has_side_effects=True
         ),
         name="long_conv",
     )(

time: 89.3 us -> 86.7 us (0.971)
  local copies, waits for them, and re-layouts: 9.94 us -> 2.06 us
  Pallas kernels: 77.2 us -> 80.5 us
  matrix products: 0.62 us -> 1.97 us
    unnamed x25 -> x17, local copies, waits for them, and re-layouts: 9.1 us -> 1.21 us
    pallas_call x1, Pallas kernels: 29.9 us -> 33.2 us  [short_window(): pl.pallas_call(conv_kernel, out_shape=(jax.ShapeDtypeStruct(key_feat.shap...]
    dot_general x1, matrix products: 0.62 us -> 1.97 us  [body(): embedded = jnp.dot(onehot, embed_table, preferred_element_type=jnp.float32)]
where the time goes in v4:
time: 86.7 us; the launch traced here: 86.5 us
  Pallas kernels  80.5 us (93%)
  local copies, waits for them, and re-layouts  2.06 us (2%)
  matrix products  1.97 us (2%)
  other arithmetic  1.88 us (2%)
    pallas_call x1, Pallas kernels, mlp(): pl.pallas_call(functools.partial(mlp_kernel, local), out_shape=jax.ShapeD...  47.3 us
    pallas_call x1, Pallas kernels, short_window(): pl.pallas_call(conv_kernel, out_shape=(jax.ShapeDtypeStruct(key_feat.shap...  33.2 us
    dot_general x1, matrix products, body(): embedded = jnp.dot(onehot, embed_table, preferred_element_type=jnp.float32)  1.97 us
    concatenate x1, other arithmetic, body(): jnp.concatenate([circulant_up.reshape(-1, BLOCK), circulant_down.reshape(...  1.88 us

profile of v4, /device:TPU:0, one launch (start us, length us, event | category | flops | bytes accessed | tf_op | source)
XLA Modules:
  0.0 86.5 jit_solution(15545662007997270461)
XLA Ops:
  0.0 0.0 copy-start
  0.0 0.8 reshape.22
  0.8 1.9 %fusion.2.cols_ref = bf16[544,512]{1,0:T(8,128)(2,1)} fusion(bf16[4,512]{1,0:T(4,128)(2,1)S(1)} %reshape.22, bf16[256,512]{1,0:T(8,128)(2,1)} %bitcast.9, bf16[256,512]{1,0:T(8,128)(2,1)} %bitcast.10), kind=kLoop, calls=%fused_computation.4 | loop fusion | flops 2228224 | bytes 1085440 | tf_op jit(solution)/shard_map/concatenate | solution.py:602
  2.7 0.0 copy-start.5
  2.7 0.0 copy-start.6
  2.7 0.0 copy-start.7
  2.7 33.2 %long_conv.1 = (bf16[128,2048]{1,0:T(8,128)(2,1)}, bf16[128,2048]{1,0:T(8,128)(2,1)}, bf16[4,544,512]{2,1,0:T(8,128)(2,1)}) custom-call(bf16[128,2048]{1,0:T(8,128)(2,1)} %key_ref.1, bf16[128,2048]{1,0:T(8,128)(2,1)} %value_ref.1, bf16[128,2048]{1,0:T(8,128)(2,1)} %filter_ref.1, bf16[2048,1024]{1,0:T(8,128)(2,1)} %constant.16.clone.fwd_hbm, ...), custom_call_target="tpu_custom_call" | custom-call | tf_op jit(solution)/shard_map/long_conv/pallas_call | solution.py:316
  35.9 0.0 copy-done
  35.9 0.0 copy-done.5
  36.0 0.0 copy-done.6
  36.0 0.0 copy-done.7
  36.0 0.0 copy-start.1
  36.0 0.0 copy-start.2
  36.0 0.0 copy-start.3
  36.0 0.0 copy-start.4
  36.0 2.0 %fusion = bf16[128,2048]{1,0:T(8,128)(2,1)S(1)} fusion(bf16[512,2048]{1,0:T(8,128)(2,1)S(1)} %copy-done, bf16[128,2048]{1,0:T(8,128)(2,1)} %get-tuple-element.9, bf16[128,2048]{1,0:T(8,128)(2,1)} %get-tuple-element.8, bf16[128,2048]{1,0:T(8,128)(2,1)S(1)} %copy-done.5, f32[2048]{0:T(1024)S(1)} %copy-done.6, s32[128]{0:T(128)S(1)} %copy-done.7), kind=kOutput, calls=%fused_computation.1 | convolution fusion | flops 270598144 | bytes 4203008 | tf_op jit(solution)/shard_map/dot_general | solution.py:608
  38.0 0.0 copy-done.1
  38.0 0.1 copy-done.2
  38.1 0.1 copy-done.3
  38.2 0.2 copy-done.4
  38.4 47.3 %circulant_mlp.1 = bf16[4,32,2048]{2,1,0:T(8,128)(2,1)S(1)} custom-call(bf16[4,32,2048]{2,1,0:T(8,128)(2,1)S(1)} %bitcast.7, bf16[2176,512]{1,0:T(8,128)(2,1)S(1)} %bitcast.6, bf16[512,512]{1,0:T(8,128)(2,1)S(1)} %copy-done.4, bf16[512,512]{1,0:T(8,128)(2,1)S(1)} %copy-done.3, bf16[512,768]{1,0:T(8,128)(2,1)S(1)} %copy-done.2), custom_call_target="tpu_custom_call" | custom-call | tf_op jit(solution)/shard_map/circulant_mlp/pallas_call | solution.py:552
  85.7 0.8 copy.17
Async XLA Ops:
  0.0 35.9 %copy-start = (bf16[512,2048]{1,0:T(8,128)(2,1)S(1)}, bf16[512,2048]{1,0:T(8,128)(2,1)}, u32[]{:S(2)}) copy-start(bf16[512,2048]{1,0:T(8,128)(2,1)} %param.16) | copy-start | bytes 6291460
  2.7 33.2 %copy-start.5 = (bf16[128,2048]{1,0:T(8,128)(2,1)S(1)}, bf16[128,2048]{1,0:T(8,128)(2,1)}, u32[]{:S(2)}) copy-start(bf16[128,2048]{1,0:T(8,128)(2,1)} %param.17) | copy-start | bytes 1572868
  2.7 33.2 %copy-start.6 = (f32[2048]{0:T(1024)S(1)}, f32[2048]{0:T(1024)}, u32[]{:S(2)}) copy-start(f32[2048]{0:T(1024)} %param.21) | copy-start | bytes 24580
  2.7 33.2 %copy-start.7 = (s32[128]{0:T(128)S(1)}, s32[128]{0:T(128)}, u32[]{:S(2)}) copy-start(s32[128]{0:T(128)} %param.15) | copy-start | bytes 1540
  36.0 2.0 %copy-start.1 = (bf16[4,544,512]{2,1,0:T(8,128)(2,1)S(1)}, bf16[4,544,512]{2,1,0:T(8,128)(2,1)}, u32[]{:S(2)}) copy-start(bf16[4,544,512]{2,1,0:T(8,128)(2,1)} %get-tuple-element.10) | copy-start | bytes 6684676
  36.0 2.1 %copy-start.2 = (bf16[512,768]{1,0:T(8,128)(2,1)S(1)}, bf16[512,768]{1,0:T(8,128)(2,1)}, u32[]{:S(2)}) copy-start(bf16[512,768]{1,0:T(8,128)(2,1)} %constant.15.clone.tap_ref) | copy-start | bytes 2359300
  36.0 2.2 %copy-start.3 = (bf16[512,512]{1,0:T(8,128)(2,1)S(1)}, bf16[512,512]{1,0:T(8,128)(2,1)}, u32[]{:S(2)}) copy-start(bf16[512,512]{1,0:T(8,128)(2,1)} %constant.14.clone.inv_ref) | copy-start | bytes 1572868
  36.0 2.4 %copy-start.4 = (bf16[512,512]{1,0:T(8,128)(2,1)S(1)}, bf16[512,512]{1,0:T(8,128)(2,1)}, u32[]{:S(2)}) copy-start(bf16[512,512]{1,0:T(8,128)(2,1)} %constant.13.clone.fwd_ref) | copy-start | bytes 1572868
